TPU v7x, 256 devices: a whole 4x4x8 slice. The times are simulated.
256 devices in a mesh: ctx: 64 (over y, z, core), head: 4 (over x).
Axes of the slice: x: 4, y: 4, z: 8, core: 2. Of those that a mesh axis runs over, the one named last changes fastest.
Arguments:
- normed_layer_input: bfloat16 [8192, 4096], P('ctx', 'head'), may hold values from -6 to 6
- mix: float32 [4096], P('head'), may hold values from 0.1 to 0.9
- paired_down_weight: bfloat16 [4096, 256], P('head'), may hold values from -0.09375 to 0.09375
- decay_up_weight: bfloat16 [128, 4096], P(None, 'head'), may hold values from -2 to 2
- rate_up_weight: bfloat16 [128, 4096], P(None, 'head'), may hold values from -1 to 1
- decay_bias: float32 [4096], P('head'), may hold values from -13 to -2.5
- rate_bias: float32 [4096], P('head'), may hold values from -11 to 1
- recept: bfloat16 [8192, 4096], P('ctx', 'head'), may hold values from -6 to 6
- key: bfloat16 [8192, 4096], P('ctx', 'head'), may hold values from -6 to 6
- value: bfloat16 [8192, 4096], P('ctx', 'head'), may hold values from -6 to 6
- window_state_start: float32 [64, 64, 64], P('head'), may hold values from -160 to 160
Outputs:
- mixed_out: bfloat16 [8192, 4096], P('ctx', 'head')
All inputs are finite; a program needn't handle non-finite values.
Results may differ from a plain program's by a relative error of at most 0.0025.
Values may be sent and summed in bfloat16 or wider, within the bound.
A program may use at most 192 MiB of HBM per device.

v0:
```python
import jax
import jax.numpy as jnp
from jax import lax
from jax.sharding import PartitionSpec as P

SPAN = 64


def from_behind(block, axis, distance):
    devices = range(lax.axis_size(axis))
    route = [(i - distance, i) for i in devices if i - distance in devices]
    return lax.ppermute(block, axis, route)


def entering(value, axis, join, neutral):
    count, mine = (lax.axis_size(axis), lax.axis_index(axis))
    pieces = jax.tree.map(lambda part: lax.all_gather(part, axis), value)
    so_far = jax.tree.map(
        lambda part, zero: jnp.full_like(part, 0) + jnp.asarray(zero, part.dtype), value, neutral
    )

    def turn(position, so_far):
        longer = join(so_far, jax.tree.map(lambda part: part[position], pieces))
        return jax.tree.map(lambda new, old: jnp.where(position < mine, new, old), longer, so_far)

    return lax.fori_loop(0, count - 1, turn, so_far)


def activate(grand_total, rank):
    return jnp.concatenate([jnp.tanh(grand_total[:, :rank]), grand_total[:, rank:]], axis=1).astype(
        jnp.bfloat16
    )


def product(form, left, right):
    return jnp.einsum(form, left, right, precision=lax.Precision.HIGHEST)


def compose(earlier, later):
    return (
        product("...jl,...lk->...jk", later[0], earlier[0]),
        product("...jl,...li->...ji", later[0], earlier[1]) + later[1],
    )


def apply_map(trans, added, state):
    return product("hjl,hli->hji", trans, state) + added


def on_device(
    normed_layer_input,
    mix,
    paired_down_weight,
    decay_up_weight,
    rate_up_weight,
    decay_bias,
    rate_bias,
    recept,
    key,
    value,
    window_state_start,
):
    rows, width = normed_layer_input.shape
    heads, size = (window_state_start.shape[0], window_state_start.shape[1])
    rank = decay_up_weight.shape[0]
    last = from_behind(normed_layer_input[rows - 1 :], "ctx", 1)
    before = jnp.concatenate([last, normed_layer_input[: rows - 1]], axis=0)
    xf = normed_layer_input.astype(jnp.float32)
    token_shifted = (xf + (before.astype(jnp.float32) - xf) * mix).astype(jnp.bfloat16)
    running_sum = jnp.dot(token_shifted, paired_down_weight, preferred_element_type=jnp.float32)
    hidden = activate(lax.psum(running_sum, "head"), rank)
    decay_logarithm = -0.606531 * jax.nn.sigmoid(
        decay_bias + jnp.dot(hidden[:, :rank], decay_up_weight, preferred_element_type=jnp.float32)
    )
    learning_rate_value = jax.nn.sigmoid(
        rate_bias + jnp.dot(hidden[:, rank:], rate_up_weight, preferred_element_type=jnp.float32)
    )
    spans = rows // SPAN
    shape4 = (spans, SPAN, heads, size)
    decay_logarithm = decay_logarithm.reshape(shape4)
    kf = key.astype(jnp.float32).reshape(shape4)
    vf = value.astype(jnp.float32).reshape(shape4)
    rf = recept.astype(jnp.float32).reshape(shape4)
    direction = kf / jnp.sqrt(jnp.sum(kf * kf, axis=-1, keepdims=True) + 1e-06)
    removal = learning_rate_value.reshape(shape4) * direction
    cumul = jnp.cumsum(decay_logarithm, axis=1)
    prior = cumul - decay_logarithm
    final = cumul[:, SPAN - 1 :]
    dir_in = direction * jnp.exp(prior)
    read_in = rf * jnp.exp(cumul)
    key_out = kf * jnp.exp(-cumul)
    rem_out = removal * jnp.exp(-cumul)
    key_end = kf * jnp.exp(final - cumul)
    rem_end = removal * jnp.exp(final - cumul)
    places = jnp.arange(SPAN)
    strict = (places[:, None] > places[None, :]).astype(jnp.float32)
    upto = (places[:, None] >= places[None, :]).astype(jnp.float32)
    a_kk = product("nthj,nshj->nhts", dir_in, key_out) * strict
    a_kb = product("nthj,nshj->nhts", dir_in, rem_out) * strict
    a_rk = product("nthj,nshj->nhts", read_in, key_out) * upto
    a_rb = product("nthj,nshj->nhts", read_in, rem_out) * upto
    right_side = jnp.concatenate(
        [dir_in.transpose(0, 2, 1, 3), product("nhts,nshi->nhti", a_kk, vf)], axis=-1
    )
    system = jnp.eye(SPAN, dtype=jnp.float32) + a_kb
    solved = jax.scipy.linalg.solve_triangular(system, right_side, lower=True, unit_diagonal=True)
    weight_q = solved[..., :size]
    base_h = solved[..., size:]
    trans = jnp.exp(final[:, 0])[:, :, :, None] * jnp.eye(size, dtype=jnp.float32) - product(
        "nshj,nhsl->nhjl", rem_end, weight_q
    )
    added = product("nshj,nshi->nhji", key_end, vf) - product("nshj,nhsi->nhji", rem_end, base_h)
    prefix_m, prefix_u = lax.associative_scan(compose, (trans, added), axis=0)
    total_m = prefix_m[spans - 1]
    total_u = prefix_u[spans - 1]
    identity = jnp.broadcast_to(jnp.eye(size, dtype=jnp.float32), (heads, size, size))
    before_m, before_u = entering(
        (total_m, total_u), "ctx", compose, (identity, jnp.zeros_like(total_u))
    )
    start = apply_map(before_m, before_u, window_state_start)
    after = product("nhjl,hli->nhji", prefix_m, start) + prefix_u
    starts = jnp.concatenate([start[None], after[: spans - 1]], axis=0)
    full_h = base_h + product("nhtl,nhli->nhti", weight_q, starts)
    reads = (
        product("nthj,nhji->nthi", read_in, starts)
        + product("nhts,nshi->nthi", a_rk, vf)
        - product("nhts,nhsi->nthi", a_rb, full_h)
    )
    mean = jnp.mean(reads, axis=-1, keepdims=True)
    centered = reads - mean
    var = jnp.mean(centered * centered, axis=-1, keepdims=True)
    normed = (centered / jnp.sqrt(var + 0.00064)).astype(jnp.bfloat16)
    return normed.reshape(rows, width)


def solution(mesh):
    in_specs = (
        P("ctx", "head"),
        P("head"),
        P("head", None),
        P(None, "head"),
        P(None, "head"),
        P("head"),
        P("head"),
        P("ctx", "head"),
        P("ctx", "head"),
        P("ctx", "head"),
        P("head", None, None),
    )
    out_specs = P("ctx", "head")
    return jax.shard_map(
        on_device, mesh=mesh, in_specs=in_specs, out_specs=out_specs, check_vma=False
    )
```

profile of v0, /device:TPU:25, one launch (start us, length us, event | category | flops | bytes accessed | tf_op | source)
XLA Modules:
  0.0 794.4 jit_solution(12532157890499619942)
XLA Ops:
  7.3 4.1 collective-permute-start
  13.8 2.2 fusion.55
  17.9 44.8 %all-reduce.6.cloned.1.call-done = f32[128,256]{1,0:T(8,128)} async-done(((f32[128,256]{1,0:T(8,128)}), f32[128,256]{1,0:T(8,128)}) %all-reduce.6.cloned.1.call-update) | async-done | bytes 131088 | tf_op jit(solution)/shard_map/psum | solution.py:71
  66.5 2.0 fusion.25
  68.6 2.3 reshape.103
  70.9 4.1 fusion.42
  75.0 3.4 convolution_multiply_fusion.2
  78.4 3.5 fusion.16
  81.9 158.7 %custom-call.4 = f32[2,16,1,64,64]{3,4,2,1,0:T(8,128)} custom-call(f32[2,16,1,64,64]{4,3,2,1,0:T(8,128)} %fusion.16), custom_call_target="InvertDiagBlocksLowerTriangular" | custom-call | tf_op jit(solution)/shard_map/jit(_solve_triangular)/vmap(vmap())/triangular_solve | solution.py:106
  240.5 2.2 fusion.79
  242.7 3.7 fusion.27
  247.4 3.3 convolution_subtract_fusion.1
  255.9 3.7 convolution_subtract_fusion
  259.6 1.9 fusion.26
  266.0 2.7 convolution_multiply_fusion.1
  268.7 3.1 convolution_bitcast_fusion.2
  271.8 4.3 convolution_multiply_fusion
  276.1 121.8 %all-gather.3.cloned.1.call-done = f32[64,16,64,64]{3,2,1,0:T(8,128)} async-done(((f32[1,16,64,64]{3,2,1,0:T(8,128)}), f32[64,16,64,64]{3,2,1,0:T(8,128)}) %all-gather.3.cloned.1.call-update) | async-done | bytes 16777232 | tf_op jit(solution)/shard_map/all_gather | solution.py:17
  397.9 142.7 %all-gather.5.cloned.1.call-done = f32[64,16,64,64]{3,2,1,0:T(8,128)} async-done(((f32[1,16,64,64]{3,2,1,0:T(8,128)}), f32[64,16,64,64]{3,2,1,0:T(8,128)}) %all-gather.5.cloned.1.call-update) | async-done | bytes 16777232 | tf_op jit(solution)/shard_map/all_gather | solution.py:17
  540.6 233.2 %while.16 = (s32[]{:T(128)}, f32[16,64,64]{2,1,0:T(8,128)S(1)}, f32[16,64,64]{2,1,0:T(8,128)S(1)}, s32[]{:T(128)}, f32[64,16,64,64]{3,2,1,0:T(8,128)}, /*index=5*/f32[64,16,64,64]{3,2,1,0:T(8,128)}, s32[]{:T(128)}, s32[]{:T(128)}) while((s32[]{:T(128)}, f32[16,64,64]{2,1,0:T(8,128)S(1)}, f32[16,64,64]{2,1,0:T(8,128)S(1)}, ...), condition=%wide.region_4.5_spmd.clone, body=%wide.region_3.4_spmd.clone.sunk | while | flops 100990976 | bytes 5245556 | solution.py:26
  542.7 1.9 fusion.109
  774.5 2.2 convolution_bitcast_fusion.3
  779.1 3.6 fusion.12
  782.8 3.2 fusion.77
  (319 shorter events, 252.1 us)
Async XLA Ops:
  6.5 767.3 %copy-start = (f32[16,64,64]{2,1,0:T(8,128)S(1)}, f32[16,64,64]{2,1,0:T(8,128)}, u32[]{:S(2)}) copy-start(f32[16,64,64]{2,1,0:T(8,128)} %param.23) | copy-start | bytes 786436
  6.5 256.8 %copy-start.12 = (bf16[128,1024]{1,0:T(8,128)(2,1)S(1)}, bf16[128,1024]{1,0:T(8,128)(2,1)}, u32[]{:S(2)}) copy-start(bf16[128,1024]{1,0:T(8,128)(2,1)} %param.20) | copy-start | bytes 786436
  6.5 56.1 %all-reduce.6.cloned.1.call-start = ((), (), s32[]{:S(2)}) async-start(), calls=%async_computation | async-start | bytes 262144 | tf_op jit(solution)/shard_map/psum | solution.py:71
  7.3 6.4 collective-permute-start
  16.0 381.9 %all-gather.3.cloned.1.call-start = ((), (), s32[]{:S(2)}) async-start(), calls=%async_computation.1 | async-start | bytes 34078720 | tf_op jit(solution)/shard_map/all_gather | solution.py:17
  17.9 245.4 %copy-start.7 = (bf16[2,64,16,64]{1,3,2,0:T(8,128)(2,1)}, bf16[2,64,16,64]{1,3,2,0:T(8,128)(2,1)S(1)}, u32[]{:S(2)}) copy-start(bf16[2,64,16,64]{1,3,2,0:T(8,128)(2,1)S(1)} %copy.94) | copy-start | bytes 786436
  75.0 3.4 copy-start.4
  75.0 3.4 copy-start.5
  246.4 1.0 copy-start.1
  250.6 1.0 copy-start.6
  251.6 0.8 copy-start.9
  252.5 0.8 copy-start.8
  254.2 286.4 %all-gather.5.cloned.1.call-start = ((), (), s32[]{:S(2)}) async-start(), calls=%async_computation.2 | async-start | bytes 34078720 | tf_op jit(solution)/shard_map/all_gather | solution.py:17
  259.6 1.9 copy-start.11
  261.6 0.8 copy-start.10
  266.0 5.8 copy-start.3
  268.7 509.2 %copy-start.2 = (f32[2,16,64,128]{3,2,1,0:T(8,128)S(1)}, f32[2,16,64,128]{3,2,1,0:T(8,128)}, u32[]{:S(2)}) copy-start(f32[2,16,64,128]{3,2,1,0:T(8,128)} %copy-done.1) | copy-start | bytes 3145732
Sparse Core Ops, SparseCore 0:
  16.1 46.5 all-reduce.5
  254.3 143.5 all-gather.2
  401.1 139.4 all-gather.4
where the time goes:
time: 803 us; the launch traced here: 794 us
  waiting for transfers between devices  309 us (38%)
  matrix products  274 us (34%)
  other arithmetic  170 us (21%)
  local copies, waits for them, and re-layouts  19.3 us (2%)
  between operations  13.5 us (2%)
    dot_general x142, matrix products, product(): return jnp.einsum(form, left, right, precision=lax.Precision.HIGHEST)  265 us
    all_gather x2, waiting for transfers between devices, entering(): pieces = jax.tree.map(lambda part: lax.all_gather(part, axis), value)  265 us
    another operation x3, other arithmetic, on_device(): jax.scipy.linalg.solve_triangular(system, right_side, lower=True, unit_di...  159 us
    psum x1, waiting for transfers between devices, on_device(): hidden = activate(lax.psum(running_sum, 'head'), rank)  44.8 us
  transfers between devices with their start and end apart: 4, of which 3 were waited for; matrix products, arithmetic and copies ran while one was open for 3% of the time, Pallas kernels for 0%

commit v1 on v0

v1 whole, which is shorter than its diff:
```python
import functools
import jax
import jax.numpy as jnp
from jax import lax
from jax.experimental import pallas as pl
from jax.experimental.pallas import tpu as pltpu

F32 = jnp.float32
BF16 = jnp.bfloat16
NN = (((1,), (0,)), ((), ()))
NT = (((1,), (1,)), ((), ()))


def dot(a, b, dims=NN):
    return lax.dot_general(a, b, dims, preferred_element_type=F32)


def split(x):
    high = x.astype(BF16)
    return high, (x - high.astype(F32)).astype(BF16)


def cat(parts, axis):
    return jnp.concatenate(parts, axis=axis)


def mm(a, b):
    ah, al = split(a)
    bh, bl = split(b)
    side = cat([bh, bl], 1)
    both = dot(cat([ah, al], 1), cat([side, side], 0))
    n = b.shape[1]
    return both[:, :n] + both[:, n:]


def mm3(a, b):
    ah, al = split(a)
    bh, bl = split(b)
    return dot(cat([ah, al], 1), cat([bh, bh], 0)) + dot(ah, bl)


def iota(shape, axis):
    return lax.broadcasted_iota(jnp.int32, shape, axis)


def chunk_kernel(hid, du, ru, db, rb, rec, key, val, mu_out, reff_out, base_out, *, pairs):
    T = hid.shape[0]
    row, col = iota((T, T), 0), iota((T, T), 1)
    tri = (row >= col).astype(BF16)
    half = (row // 64 == col // 64).astype(BF16)
    eye = (row == col).astype(F32)
    first = iota((T, 128), 1) < 64
    first2 = cat([first, first], 1)
    hd, hr = hid[:, :128], hid[:, 128:]
    tri2, half2 = cat([tri, tri], 1), cat([half, half], 0)
    P = range(pairs)
    H = range(2 * pairs)
    at = [slice(128 * p, 128 * p + 128) for p in P]

    logd = [-0.606531 * jax.nn.sigmoid(dot(hd, du[:, at[p]]) + db[:, at[p]]) for p in P]
    rate = [jax.nn.sigmoid(dot(hr, ru[:, at[p]]) + rb[:, at[p]]) for p in P]
    cum = []
    for p in P:
        l1, rest = split(logd[p])
        r1 = logd[p] - l1.astype(F32)
        l3 = (r1 - rest.astype(F32)).astype(BF16)
        cum.append(dot(tri2, cat([l1, rest], 0)) + dot(tri, l3))
    kf = [key[:, at[p]].astype(F32) for p in P]
    square = [dot(cat(split(kf[p] * kf[p]), 1), half2) for p in P]
    direction = [kf[p] * lax.rsqrt(square[p] + 1e-06) for p in P]
    mid = [cum[p][63:64] for p in P]
    last = [cum[p][T - 1 :] for p in P]
    e_in = [jnp.exp(cum[p] - mid[p]) for p in P]
    e_prior = [jnp.exp(cum[p] - logd[p] - mid[p]) for p in P]
    e_out = [jnp.exp(mid[p] - cum[p]) for p in P]
    dir_in = [direction[p] * e_prior[p] for p in P]
    read_in = [rec[:, at[p]].astype(F32) * e_in[p] for p in P]
    key_out = [kf[p] * e_out[p] for p in P]
    rem_out = [rate[p] * direction[p] * e_out[p] for p in P]
    e_mid = [jnp.exp(mid[p]) for p in P]
    e_end = [jnp.exp(last[p] - mid[p]) for p in P]
    e_all = [jnp.exp(last[p]) for p in P]

    scores = []
    zero = jnp.zeros((2 * T, 128), BF16)
    keep = cat([first, first], 0)
    for p in P:
        xh, xl = split(cat([dir_in[p], read_in[p]], 0))
        yh, yl = split(cat([key_out[p], rem_out[p]], 0))
        yhh = cat([yh, yh], 1)
        for side in (0, 1):
            pick = keep if side == 0 else jnp.logical_not(keep)
            xhs, xls = jnp.where(pick, xh, zero), jnp.where(pick, xl, zero)
            scores.append(dot(cat([xhs, xls], 1), yhh, NT) + dot(xhs, yl, NT))
    strict = row > col
    upto = row >= col
    a_kk = [jnp.where(strict, scores[h][:T, :T], 0.0) for h in H]
    low = [jnp.where(strict, scores[h][:T, T:], 0.0) for h in H]
    a_rk = [jnp.where(upto, scores[h][T:, :T], 0.0) for h in H]
    a_rb = [jnp.where(upto, scores[h][T:, T:], 0.0) for h in H]

    block = row // 8 == col // 8
    d = [jnp.where(block, low[h], 0.0) for h in H]
    d2 = [mm(d[h], d[h]) for h in H]
    dd = [mm(cat([d[h], d2[h]], 0), d2[h]) for h in H]
    poly = [eye - d[h] + d2[h] - dd[h][:T] for h in H]
    inv = [poly[h] + mm(poly[h], dd[h][T:]) for h in H]
    size = 8
    while size < T:
        pair_mask = (row // (2 * size) == col // (2 * size)) & (row // size > col // size)
        step = [mm(jnp.where(pair_mask, low[h], 0.0), inv[h]) for h in H]
        inv = [inv[h] - mm(inv[h], step[h]) for h in H]
        size *= 2

    vals = [val[:, at[p]] for p in P]
    kv = [dot(cat(split(a_kk[h]), 1), cat([vals[h // 2]] * 2, 0)) for h in H]
    right = [
        cat([dir_in[p] * e_mid[p], jnp.where(first, kv[2 * p], kv[2 * p + 1])], 1) for p in P
    ]
    sol = [mm3(inv[h], right[h // 2]) for h in H]
    solved = [jnp.where(first2, sol[2 * p], sol[2 * p + 1]) for p in P]
    for p in P:
        wide = cat([solved[p], cat([jnp.zeros((T, 128), F32), vals[p].astype(F32)], 1)], 0)
        ends = cat([-rem_out[p] * e_end[p], key_out[p] * e_end[p]], 0).T
        left = cat(
            [ends] + [cat([-a_rb[2 * p + s], a_rk[2 * p + s]], 1) for s in (0, 1)], 0
        )
        lh, ll = split(left)
        wh, wl = split(wide)
        out = dot(lh, wh) + dot(lh, wl) + dot(ll, wh)
        maps = out[:T]
        trans = maps[:, :128] + eye * e_all[p]
        added = maps[:, 128:]
        low_lane = iota((64, 128), 1) < 64
        mu_out[2 * p] = jnp.where(low_lane, trans[:64], pltpu.roll(added[:64], 64, 1))
        mu_out[2 * p + 1] = jnp.where(low_lane, pltpu.roll(trans[64:], 64, 1), added[64:])
        reads = jnp.where(first2, out[T : 2 * T], out[2 * T :])
        reff_out[:, at[p]] = read_in[p] * e_mid[p] + reads[:, :128]
        base_out[:, at[p]] = reads[:, 128:]


def chunk(hid, du, ru, db, rb, rec, key, val, pairs=2):
    T, width = rec.shape
    heads = width // 64
    w = 128 * pairs
    grid = (width // w,)
    cols = lambda i: (0, i)
    return pl.pallas_call(
        functools.partial(chunk_kernel, pairs=pairs),
        grid=grid,
        in_specs=[
            pl.BlockSpec((T, 256), lambda i: (0, 0)),
            pl.BlockSpec((128, w), cols),
            pl.BlockSpec((128, w), cols),
            pl.BlockSpec((1, w), cols),
            pl.BlockSpec((1, w), cols),
            pl.BlockSpec((T, w), cols),
            pl.BlockSpec((T, w), cols),
            pl.BlockSpec((T, w), cols),
        ],
        out_specs=[
            pl.BlockSpec((2 * pairs, 64, 128), lambda i: (i, 0, 0)),
            pl.BlockSpec((T, w), cols),
            pl.BlockSpec((T, w), cols),
        ],
        out_shape=[
            jax.ShapeDtypeStruct((heads, 64, 128), F32),
            jax.ShapeDtypeStruct((T, width), F32),
            jax.ShapeDtypeStruct((T, width), F32),
        ],
        compiler_params=pltpu.CompilerParams(vmem_limit_bytes=48 * 1024 * 1024),
    )(hid, du, ru, db, rb, rec, key, val)


MESH = pl.DeviceIdType.MESH


def hidden_kernel(
    x_ref, mix_ref, down_ref, out_ref,
    tail, total, shares, hidden, sends, recvs, *, nctx, nhead,
):
    ctx, head = lax.axis_index("ctx"), lax.axis_index("head")
    after, behind = lax.rem(ctx + 1, nctx), lax.rem(ctx + nctx - 1, nctx)
    T, width = x_ref.shape
    share = T // nhead
    barrier = pltpu.get_barrier_semaphore()
    for other in (after, behind):
        pl.semaphore_signal(barrier, inc=1, device_id={"ctx": other}, device_id_type=MESH)
    mates = [lax.rem(head + step, nhead) for step in range(1, nhead)]
    for mate in mates:
        pl.semaphore_signal(barrier, inc=1, device_id={"head": mate}, device_id_type=MESH)
    pl.semaphore_wait(barrier, 1 + nhead)

    shift = pltpu.make_async_remote_copy(
        src_ref=x_ref.at[pl.ds(T - 16, 16)],
        dst_ref=tail,
        send_sem=sends.at[0],
        recv_sem=recvs.at[0],
        device_id={"ctx": after},
        device_id_type=MESH,
    )
    shift.start()
    mix = mix_ref[...]
    xf = x_ref[...].astype(F32)
    before = pltpu.roll(xf, 1, 0)
    shifted = (xf + (before - xf) * mix).astype(BF16)
    total[...] = dot(shifted, down_ref[...])
    shift.wait()
    xt = x_ref[0:16, :].astype(F32)
    edge = jnp.where(ctx > 0, tail[...].astype(F32)[15:16], 0.0)
    before = jnp.where(iota((16, width), 0) == 0, edge, pltpu.roll(xt, 1, 0))
    shifted = (xt + (before - xt) * mix).astype(BF16)
    total[0:16, :] = dot(shifted, down_ref[...])

    copies = []
    for step, mate in enumerate(mates):
        copy = pltpu.make_async_remote_copy(
            src_ref=total.at[pl.ds(pl.multiple_of(mate * share, share), share)],
            dst_ref=shares.at[step],
            send_sem=sends.at[1 + step],
            recv_sem=recvs.at[1 + step],
            device_id={"head": mate},
            device_id_type=MESH,
        )
        copy.start()
        copies.append(copy)
    mine = pl.ds(pl.multiple_of(head * share, share), share)
    grand = total[mine, :]
    for step, copy in enumerate(copies):
        copy.wait_recv()
        grand = grand + shares[step]
    hidden[mine, :] = cat([jnp.tanh(grand[:, :128]), grand[:, 128:]], 1).astype(BF16)
    spread = []
    for step, mate in enumerate(mates):
        copy = pltpu.make_async_remote_copy(
            src_ref=hidden.at[mine],
            dst_ref=hidden.at[mine],
            send_sem=sends.at[nhead + step],
            recv_sem=recvs.at[nhead + step],
            device_id={"head": mate},
            device_id_type=MESH,
        )
        copy.start()
        spread.append(copy)
    for copy in copies:
        copy.wait_send()
    for copy in spread:
        copy.wait()
    out_ref[...] = hidden[...]


def hidden_of(x, mix, down, nctx, nhead):
    T, width = x.shape
    vmem = pl.BlockSpec(memory_space=pltpu.VMEM)
    return pl.pallas_call(
        functools.partial(hidden_kernel, nctx=nctx, nhead=nhead),
        in_specs=[vmem] * 3,
        out_specs=vmem,
        out_shape=jax.ShapeDtypeStruct((T, 256), BF16),
        scratch_shapes=[
            pltpu.VMEM((16, width), BF16),
            pltpu.VMEM((T, 256), F32),
            pltpu.VMEM((nhead - 1, T // nhead, 256), F32),
            pltpu.VMEM((T, 256), BF16),
            pltpu.SemaphoreType.DMA((2 * nhead,)),
            pltpu.SemaphoreType.DMA((2 * nhead,)),
        ],
        compiler_params=pltpu.CompilerParams(
            collective_id=0, has_side_effects=True, vmem_limit_bytes=32 * 1024 * 1024
        ),
    )(x, mix, down)


def later_of(map_later, earlier):
    wide = cat([earlier, jnp.zeros_like(earlier)], 0)
    lane = iota(map_later.shape, 1) < 64
    return mm(map_later, wide) + jnp.where(lane, 0.0, map_later)


def scan_kernel(
    mu_ref, start_ref, out_ref,
    maps, row_total, row_totals, states, got, s1, r1, s2, r2, s3, r3, *, nrow,
):
    ctx = lax.axis_index("ctx")
    n = mu_ref.shape[0]
    y, me = ctx // n, lax.rem(ctx, n)
    base = y * n
    mates = [lax.rem(me + step, n) for step in range(1, n)]
    rows = [lax.rem(y + step, nrow) for step in range(1, nrow)]
    barrier = pltpu.get_barrier_semaphore()
    for mate in mates:
        pl.semaphore_signal(barrier, inc=1, device_id={"ctx": base + mate}, device_id_type=MESH)
    for row in rows:
        pl.semaphore_signal(barrier, inc=1, device_id={"ctx": row * n + me}, device_id_type=MESH)
    pl.semaphore_wait(barrier, n + nrow - 2)

    first = []
    for step, mate in enumerate(mates):
        copy = pltpu.make_async_remote_copy(
            src_ref=mu_ref.at[mate],
            dst_ref=maps.at[me],
            send_sem=s1.at[step],
            recv_sem=r1.at[step],
            device_id={"ctx": base + mate},
            device_id_type=MESH,
        )
        copy.start()
        first.append(copy)
    maps[me] = mu_ref[me]
    for copy in first:
        copy.wait_recv()

    prefix = [maps[d] for d in range(n)]
    size = 1
    while size < n:
        for low in range(size, n, 2 * size):
            group = cat(prefix[low : low + size], 0)
            joined = later_of(group, prefix[low - 1])
            for d in range(size):
                prefix[low + d] = joined[64 * d : 64 * d + 64]
        size *= 2
    row_total[...] = prefix[n - 1]
    second = []
    for step, row in enumerate(rows):
        copy = pltpu.make_async_remote_copy(
            src_ref=row_total,
            dst_ref=row_totals.at[y],
            send_sem=s2.at[step],
            recv_sem=r2.at[step],
            device_id={"ctx": row * n + me},
            device_id_type=MESH,
        )
        copy.start()
        second.append(copy)
    row_totals[y] = row_total[...]
    for copy in second:
        copy.wait_recv()
    begin = start_ref[me]
    state = cat([begin, begin], 1)
    for row in range(nrow - 1):
        state = jnp.where(row < y, later_of(row_totals[row], state), state)
    after = later_of(cat(prefix[: n - 1], 0), state)
    lane = iota((32, 128), 1) < 64
    for d in range(n):
        full = state if d == 0 else after[64 * d - 64 : 64 * d]
        states[d] = jnp.where(lane, pltpu.roll(full[:32], 64, 1), full[32:])
    third = []
    for step, mate in enumerate(mates):
        copy = pltpu.make_async_remote_copy(
            src_ref=states.at[mate],
            dst_ref=got.at[me],
            send_sem=s3.at[step],
            recv_sem=r3.at[step],
            device_id={"ctx": base + mate},
            device_id_type=MESH,
        )
        copy.start()
        third.append(copy)
    got[me] = states[me]
    for copy in third:
        copy.wait_recv()
    out_ref[...] = got[...]
    for copy in first + second + third:
        copy.wait_send()


def starts_of(mu, start, nctx):
    n = mu.shape[0]
    nrow = nctx // n
    vmem = pl.BlockSpec(memory_space=pltpu.VMEM)
    dma = pltpu.SemaphoreType.DMA
    return pl.pallas_call(
        functools.partial(scan_kernel, nrow=nrow),
        in_specs=[vmem] * 2,
        out_specs=vmem,
        out_shape=jax.ShapeDtypeStruct((n, 32, 128), F32),
        scratch_shapes=[
            pltpu.VMEM((n, 64, 128), F32),
            pltpu.VMEM((64, 128), F32),
            pltpu.VMEM((nrow, 64, 128), F32),
            pltpu.VMEM((n, 32, 128), F32),
            pltpu.VMEM((n, 32, 128), F32),
            dma((n,)), dma((n,)), dma((nrow,)), dma((nrow,)), dma((n,)), dma((n,)),
        ],
        compiler_params=pltpu.CompilerParams(
            collective_id=1, has_side_effects=True, vmem_limit_bytes=32 * 1024 * 1024
        ),
    )(mu, start)


def read_kernel(reff, base, start, out, *, pairs):
    T = reff.shape[0]
    lane = iota((64, 128), 1) < 64
    row, col = iota((128, 128), 0), iota((128, 128), 1)
    mean64 = jnp.where(row // 64 == col // 64, 1.0 / 64, 0.0).astype(BF16)
    mean2 = cat([mean64, mean64], 0)
    for p in range(pairs):
        at = slice(128 * p, 128 * p + 128)
        a, b = start[2 * p], start[2 * p + 1]
        both_a = cat([a, pltpu.roll(a, 64, 1)], 0)
        both_b = cat([pltpu.roll(b, 64, 1), b], 0)
        state = cat([jnp.where(lane, both_a, 0.0), jnp.where(lane, 0.0, both_b)], 0)
        read = mm(reff[:, at], state) + base[:, at]
        centered = read - dot(cat(split(read), 1), mean2)
        var = dot(cat(split(centered * centered), 1), mean2)
        out[:, at] = (centered * lax.rsqrt(var + 0.00064)).astype(BF16)


def read_of(reff, base, starts, pairs=4):
    T, width = reff.shape
    w = 128 * pairs
    cols = lambda i: (0, i)
    return pl.pallas_call(
        functools.partial(read_kernel, pairs=pairs),
        grid=(width // w,),
        in_specs=[
            pl.BlockSpec((T, w), cols),
            pl.BlockSpec((T, w), cols),
            pl.BlockSpec((2 * pairs, 32, 128), lambda i: (i, 0, 0)),
        ],
        out_specs=pl.BlockSpec((T, w), cols),
        out_shape=jax.ShapeDtypeStruct((T, width), BF16),
        compiler_params=pltpu.CompilerParams(vmem_limit_bytes=32 * 1024 * 1024),
    )(reff, base, starts)


def solution(mesh):
    nctx, nhead = mesh.shape["ctx"], mesh.shape["head"]

    def on_device(x, mix, down, du, ru, db, rb, rec, key, val, start):
        hid = hidden_of(x, mix[None], down, nctx, nhead)
        mu, reff, base = chunk(hid, du, ru, db[None], rb[None], rec, key, val, pairs=4)
        starts = starts_of(mu, start, nctx)
        return read_of(reff, base, starts)

    P = jax.sharding.PartitionSpec
    both, wide = P("ctx", "head"), P("head")
    return jax.shard_map(
        on_device,
        mesh=mesh,
        in_specs=(both, wide, P("head", None), P(None, "head"), P(None, "head"), wide, wide)
        + (both,) * 3
        + (P("head", None, None),),
        out_specs=both,
        check_vma=False,
    )
```

time: 803 us -> 71.1 us (0.09)
  the two profiles are of different devices: /device:TPU:25 before, /device:TPU:1 now
where the time goes in v1:
time: 71.1 us; the launch traced here: 70.9 us
  Pallas kernels  66.2 us (93%)
  local copies, waits for them, and re-layouts  4.59 us (6%)
    pallas_call x1, Pallas kernels, starts_of(): pl.pallas_call(functools.partial(scan_kernel, nrow=nrow), in_specs=[vmem]...  36.4 us
    pallas_call x1, Pallas kernels, hidden_of(): pl.pallas_call(functools.partial(hidden_kernel, nctx=nctx, nhead=nhead),...  17.4 us
    pallas_call x1, Pallas kernels, chunk(): pl.pallas_call(functools.partial(chunk_kernel, pairs=pairs), grid=grid, i...  9.62 us
    unnamed x22, local copies, waits for them, and re-layouts  4.59 us
    pallas_call x1, Pallas kernels, read_of(): pl.pallas_call(functools.partial(read_kernel, pairs=pairs), grid=(width /...  2.76 us

profile of v1, /device:TPU:1, one launch (start us, length us, event | category | flops | bytes accessed | tf_op | source)
XLA Modules:
  0.0 70.9 jit_solution(14804100660086628882)
XLA Ops:
  0.0 0.0 copy-start.8
  0.0 0.7 copy-done.8
  0.7 0.0 copy-start
  0.7 1.0 %copy-done = bf16[1024,256]{1,0:T(8,128)(2,1)S(1)} copy-done((bf16[1024,256]{1,0:T(8,128)(2,1)S(1)}, bf16[1024,256]{1,0:T(8,128)(2,1)}, u32[]{:S(2)}) %copy-start) | copy-done | bytes 524312
  1.7 0.0 copy-start.2
  1.7 0.9 %copy-done.2 = bf16[128,1024]{1,0:T(8,128)(2,1)S(1)} copy-done((bf16[128,1024]{1,0:T(8,128)(2,1)S(1)}, bf16[128,1024]{1,0:T(8,128)(2,1)}, u32[]{:S(2)}) %copy-start.2) | copy-done | bytes 262168
  2.7 0.0 copy-start.3
  2.7 0.0 copy-start.4
  2.7 0.0 copy-start.5
  2.7 0.0 copy-start.9
  2.7 0.0 copy-start.10
  2.7 17.4 %shard_map.109.hid = bf16[128,256]{1,0:T(8,128)(2,1)S(1)} custom-call(bf16[128,1024]{1,0:T(8,128)(2,1)S(1)} %copy-done.2, f32[1,1024]{1,0:T(1,128)S(1)} %bitcast.3, bf16[1024,256]{1,0:T(8,128)(2,1)S(1)} %copy-done), custom_call_target="tpu_custom_call" | custom-call | tf_op jit(solution)/shard_map/pallas_call | solution.py:255
  20.1 0.0 copy-done.3
  20.2 0.0 copy-done.4
  20.2 0.0 copy-done.5
  20.2 0.0 copy-done.9
  20.2 0.0 copy-done.10
  20.2 0.0 copy-start.6
  20.2 0.9 %copy-done.6 = bf16[128,1024]{1,0:T(8,128)(2,1)S(1)} copy-done((bf16[128,1024]{1,0:T(8,128)(2,1)S(1)}, bf16[128,1024]{1,0:T(8,128)(2,1)}, u32[]{:S(2)}) %copy-start.6) | copy-done | bytes 262168
  21.1 0.9 %copy-done.7 = bf16[128,1024]{1,0:T(8,128)(2,1)S(1)} copy-done((bf16[128,1024]{1,0:T(8,128)(2,1)S(1)}, bf16[128,1024]{1,0:T(8,128)(2,1)}, u32[]{:S(2)}) %copy-start.7) | copy-done | bytes 262168
  22.1 9.6 %shard_map.110 = (f32[16,64,128]{2,1,0:T(8,128)S(1)}, f32[128,1024]{1,0:T(8,128)S(1)}, f32[128,1024]{1,0:T(8,128)S(1)}) custom-call(bf16[128,256]{1,0:T(8,128)(2,1)S(1)} %shard_map.109.hid, bf16[128,1024]{1,0:T(8,128)(2,1)S(1)} %copy-done.3, bf16[128,1024]{1,0:T(8,128)(2,1)S(1)} %copy-done.4, f32[1,1024]{1,0:T(1,128)S(1)} %bitcast.4, f32[1,1024]{1,0:T(1,128)S(1)} %bitcast.5, ...), custom_call_target="tpu_custom_call" | custom-call | tf_op jit(solution)/shard_map/pallas_call | solution.py:148
  31.7 0.0 copy-done.1
  31.7 36.4 %shard_map.111.start = f32[16,32,128]{2,1,0:T(8,128)S(1)} custom-call(f32[16,64,128]{2,1,0:T(8,128)S(1)} %get-tuple-element.10.mu_ref, f32[16,64,64]{2,1,0:T(8,128)S(1)} %copy-done.1), custom_call_target="tpu_custom_call" | custom-call | tf_op jit(solution)/shard_map/pallas_call | solution.py:372
  68.1 2.8 %shard_map.112 = bf16[128,1024]{1,0:T(8,128)(2,1)} custom-call(f32[128,1024]{1,0:T(8,128)S(1)} %get-tuple-element.8.reff, f32[128,1024]{1,0:T(8,128)S(1)} %get-tuple-element.9.base, f32[16,32,128]{2,1,0:T(8,128)S(1)} %shard_map.111.start), custom_call_target="tpu_custom_call" | custom-call | tf_op jit(solution)/shard_map/pallas_call | solution.py:413
  (2 shorter events, 0.0 us)
Async XLA Ops:
  0.0 0.7 copy-start.8
  0.7 1.0 %copy-start = (bf16[1024,256]{1,0:T(8,128)(2,1)S(1)}, bf16[1024,256]{1,0:T(8,128)(2,1)}, u32[]{:S(2)}) copy-start(bf16[1024,256]{1,0:T(8,128)(2,1)} %down_ref.1) | copy-start | bytes 1572868
  1.7 0.9 %copy-start.2 = (bf16[128,1024]{1,0:T(8,128)(2,1)S(1)}, bf16[128,1024]{1,0:T(8,128)(2,1)}, u32[]{:S(2)}) copy-start(bf16[128,1024]{1,0:T(8,128)(2,1)} %x_ref.1) | copy-start | bytes 786436
  2.7 17.5 %copy-start.3 = (bf16[128,1024]{1,0:T(8,128)(2,1)S(1)}, bf16[128,1024]{1,0:T(8,128)(2,1)}, u32[]{:S(2)}) copy-start(bf16[128,1024]{1,0:T(8,128)(2,1)} %du.1) | copy-start | bytes 786436
  2.7 17.5 %copy-start.4 = (bf16[128,1024]{1,0:T(8,128)(2,1)S(1)}, bf16[128,1024]{1,0:T(8,128)(2,1)}, u32[]{:S(2)}) copy-start(bf16[128,1024]{1,0:T(8,128)(2,1)} %ru.1) | copy-start | bytes 786436
  2.7 17.5 %copy-start.5 = (bf16[128,1024]{1,0:T(8,128)(2,1)S(1)}, bf16[128,1024]{1,0:T(8,128)(2,1)}, u32[]{:S(2)}) copy-start(bf16[128,1024]{1,0:T(8,128)(2,1)} %rec.1) | copy-start | bytes 786436
  2.7 17.5 %copy-start.9 = (f32[1024]{0:T(1024)S(1)}, f32[1024]{0:T(1024)}, u32[]{:S(2)}) copy-start(f32[1024]{0:T(1024)} %param.16) | copy-start | bytes 12292
  2.7 17.5 %copy-start.10 = (f32[1024]{0:T(1024)S(1)}, f32[1024]{0:T(1024)}, u32[]{:S(2)}) copy-start(f32[1024]{0:T(1024)} %param.17) | copy-start | bytes 12292
  20.2 1.0 %copy-start.6 = (bf16[128,1024]{1,0:T(8,128)(2,1)S(1)}, bf16[128,1024]{1,0:T(8,128)(2,1)}, u32[]{:S(2)}) copy-start(bf16[128,1024]{1,0:T(8,128)(2,1)} %key.1) | copy-start | bytes 786436
  21.1 0.9 %copy-start.7 = (bf16[128,1024]{1,0:T(8,128)(2,1)S(1)}, bf16[128,1024]{1,0:T(8,128)(2,1)}, u32[]{:S(2)}) copy-start(bf16[128,1024]{1,0:T(8,128)(2,1)} %val.1) | copy-start | bytes 786436
  22.1 9.6 %copy-start.1 = (f32[16,64,64]{2,1,0:T(8,128)S(1)}, f32[16,64,64]{2,1,0:T(8,128)}, u32[]{:S(2)}) copy-start(f32[16,64,64]{2,1,0:T(8,128)} %start_ref.1) | copy-start | bytes 786436

commit v2 on v0

v2 whole, which is shorter than its diff:
```python
import functools
import jax
import jax.numpy as jnp
from jax import lax
from jax.experimental import pallas as pl
from jax.experimental.pallas import tpu as pltpu

F32 = jnp.float32
BF16 = jnp.bfloat16
NN = (((1,), (0,)), ((), ()))
NT = (((1,), (1,)), ((), ()))


def dot(a, b, dims=NN):
    return lax.dot_general(a, b, dims, preferred_element_type=F32)


def split(x):
    high = x.astype(BF16)
    return high, (x - high.astype(F32)).astype(BF16)


def cat(parts, axis):
    return jnp.concatenate(parts, axis=axis)


def mm3(a, b):
    ah, al = split(a)
    bh, bl = split(b)
    return dot(cat([ah, al], 1), cat([bh, bh], 0)) + dot(ah, bl)


def iota(shape, axis):
    return lax.broadcasted_iota(jnp.int32, shape, axis)


MESH = pl.DeviceIdType.MESH
PAIRS = 4


def half_roll(x):
    return pltpu.roll(x, 64, 1)


def later_of(map_later, earlier):
    wide = cat([earlier, jnp.zeros_like(earlier)], 0)
    lane = iota(map_later.shape, 1) < 64
    return mm3(map_later, wide) + jnp.where(lane, 0.0, map_later)


def pack_state(full):
    lane = iota((32, 128), 1) < 64
    return jnp.where(lane, half_roll(full[:32]), full[32:])


def unit_inverse(low, row, col):
    T = low[0].shape[0]
    eye = (row == col).astype(F32)
    block = row // 8 == col // 8
    d = [jnp.where(block, a, 0.0) for a in low]
    d2 = [mm3(a, a) for a in d]
    dd = [mm3(cat([a, b], 0), b) for a, b in zip(d, d2)]
    poly = [eye - a + b - c[:T] for a, b, c in zip(d, d2, dd)]
    inv = [a + mm3(a, c[T:]) for a, c in zip(poly, dd)]
    size = 8
    while size < T:
        blocks = T // size

        def rows_of(a, odd):
            return [a[size * i : size * i + size] for i in range(odd, blocks, 2)]

        below = cat(rows_of(row, 1), 0) // size - 1 == cat(rows_of(col, 1), 0) // size
        step = [
            mm3(jnp.where(below, cat(rows_of(a, 1), 0), 0.0), b) for a, b in zip(low, inv)
        ]
        new = []
        for a, b in zip(inv, step):
            parts = [b[size * (i // 2) : size * (i // 2) + size] for i in range(blocks)]
            odd = cat(rows_of(a, 1), 0)
            odd = odd - mm3(odd, cat(parts, 0))
            merged = []
            for i, even in enumerate(rows_of(a, 0)):
                merged += [even, odd[size * i : size * i + size]]
            new.append(cat(merged, 0))
        inv = new
        size *= 2
    return inv


def mixed_kernel(
    x_h, mix_h, down_h, du_h, ru_h, db_h, rb_h, rec_h, key_h, val_h, start_h,
    out,
    x_ref, mix_ref, down_ref, du, ru, db, rb, rec, key, val, start_ref, loads,
    tail, total, shares, hidden, sends, recvs,
    unit, mu, left_ref, solved_ref, reff, base_ref, starts,
    sib, first_maps, chip_maps, maps, row_total, row_totals, states, got, give,
    s0, r0, s1, r1, s2, r2, s3, r3, s4, r4,
    *, nctx, nhead,
):
    ctx, head = lax.axis_index("ctx"), lax.axis_index("head")
    T, width = x_ref.shape
    n = mu.shape[0] * mu.shape[1]
    chips = n // 2
    quarter = chips // 2
    nrow = nctx // n
    y, me = ctx // n, lax.rem(ctx, n)
    chip, core = me // 2, lax.rem(me, 2)
    other_core = 1 - core
    base = y * n
    my_slot = chip // 2 + quarter * lax.rem(chip, 2)
    my_head = core * chips + my_slot
    sibling = {"ctx": base + chip * 2 + other_core}

    fetch = []
    for i, (src, dst) in enumerate(
        [(x_h, x_ref), (mix_h, mix_ref), (down_h, down_ref), (key_h, key), (du_h, du), (ru_h, ru)]
        + [(db_h, db), (rb_h, rb), (rec_h, rec), (val_h, val), (start_h.at[my_head], start_ref)]
    ):
        copy = pltpu.make_async_copy(src, dst, loads.at[i])
        copy.start()
        fetch.append(copy)

    after, behind = lax.rem(ctx + 1, nctx), lax.rem(ctx + nctx - 1, nctx)
    mates = [lax.rem(head + step, nhead) for step in range(1, nhead)]
    far = sorted(range(1, chips), key=lambda d: -min(d, chips - d))
    others = [lax.rem(chip + step, chips) for step in far]
    rows = [lax.rem(y + step, nrow) for step in range(1, nrow)]
    barrier = pltpu.get_barrier_semaphore()
    for other in [after, behind]:
        pl.semaphore_signal(barrier, inc=1, device_id={"ctx": other}, device_id_type=MESH)
    for mate in mates:
        pl.semaphore_signal(barrier, inc=1, device_id={"head": mate}, device_id_type=MESH)
    pl.semaphore_signal(barrier, inc=1, device_id=sibling, device_id_type=MESH)
    for other in [base + 2 * o + core for o in others] + [r * n + me for r in rows]:
        pl.semaphore_signal(barrier, inc=1, device_id={"ctx": other}, device_id_type=MESH)
    pl.semaphore_wait(barrier, 2 + nhead - 1 + 1 + chips - 1 + nrow - 1)

    shift = pltpu.make_async_remote_copy(
        src_ref=x_h.at[pl.ds(T - 16, 16)],
        dst_ref=tail,
        send_sem=sends.at[0],
        recv_sem=recvs.at[0],
        device_id={"ctx": after},
        device_id_type=MESH,
    )
    shift.start()
    for i in range(3):
        fetch[i].wait()
    mix = mix_ref[...]
    xf = x_ref[...].astype(F32)
    before = pltpu.roll(xf, 1, 0)
    shifted = (xf + (before - xf) * mix).astype(BF16)
    total[...] = dot(shifted, down_ref[...])
    shift.wait_recv()
    xt = x_ref[0:16, :].astype(F32)
    edge = jnp.where(ctx > 0, tail[...].astype(F32)[15:16], 0.0)
    before = jnp.where(iota((16, width), 0) == 0, edge, pltpu.roll(xt, 1, 0))
    shifted = (xt + (before - xt) * mix).astype(BF16)
    total[0:16, :] = dot(shifted, down_ref[...])

    share = T // nhead
    mine = pl.ds(pl.multiple_of(head * share, share), share)
    scatter, spread = [], []
    for step, mate in enumerate(mates):
        copy = pltpu.make_async_remote_copy(
            src_ref=total.at[pl.ds(pl.multiple_of(mate * share, share), share)],
            dst_ref=shares.at[step],
            send_sem=sends.at[1 + step],
            recv_sem=recvs.at[1 + step],
            device_id={"head": mate},
            device_id_type=MESH,
        )
        copy.start()
        scatter.append(copy)

    row, col = iota((T, T), 0), iota((T, T), 1)
    tri = (row >= col).astype(BF16)
    half = (row // 64 == col // 64).astype(BF16)
    half2 = cat([half, half], 0)
    fetch[3].wait()
    for p in range(width // 128):
        kf = key[:, 128 * p : 128 * p + 128].astype(F32)
        square = dot(cat(split(kf * kf), 1), half2)
        unit[:, 128 * p : 128 * p + 128] = kf * lax.rsqrt(square + 1e-06)

    grand = total[mine, :]
    for step, copy in enumerate(scatter):
        copy.wait_recv()
        grand = grand + shares[step]
    hidden[mine, :] = cat([jnp.tanh(grand[:, :128]), grand[:, 128:]], 1).astype(BF16)
    for step, mate in enumerate(mates):
        copy = pltpu.make_async_remote_copy(
            src_ref=hidden.at[mine],
            dst_ref=hidden.at[mine],
            send_sem=sends.at[nhead + step],
            recv_sem=recvs.at[nhead + step],
            device_id={"head": mate},
            device_id_type=MESH,
        )
        copy.start()
        spread.append(copy)
    for i in range(4, len(fetch)):
        fetch[i].wait()
    shift.wait_send()
    for copy in scatter:
        copy.wait_send()
    for copy in spread:
        copy.wait()

    eye = (row == col).astype(F32)
    first = iota((T, 128), 1) < 64
    first2 = cat([first, first], 1)
    firsts = cat([first, first], 0)
    tri2 = cat([tri, tri], 1)
    strict, upto = row > col, row >= col
    P, H = range(PAIRS), range(2 * PAIRS)

    def swap_maps(h):
        part = pl.ds(h * quarter, quarter)
        return pltpu.make_async_remote_copy(
            src_ref=mu.at[other_core, part],
            dst_ref=sib.at[part],
            send_sem=s0.at[h],
            recv_sem=r0.at[h],
            device_id=sibling,
            device_id_type=MESH,
        )

    def send_map(h, k):
        place = lax.rem(chip // 2 + k, quarter)
        to = 2 * place + h
        return to, pltpu.make_async_remote_copy(
            src_ref=chip_maps.at[h * quarter + place],
            dst_ref=maps.at[chip],
            send_sem=s1.at[h, k],
            recv_sem=r1.at[chip],
            device_id={"ctx": base + 2 * to + core},
            device_id_type=MESH,
        )

    def forward(h):
        swap_maps(h).wait_recv()
        for i in range(quarter):
            slot = h * quarter + i
            own, theirs = mu[core, slot], sib[slot]
            earlier = jnp.where(core == 0, own, theirs)
            later = jnp.where(core == 0, theirs, own)
            first_maps[slot] = earlier
            chip_maps[slot] = later_of(later, earlier)
        for k in [2, 1, 3, 0]:
            to, copy = send_map(h, k)

            @pl.when(to != chip)
            def _():
                copy.start()

    def half_of_heads(g, carry):
        def columns(ref, p):
            start = (p // 2) * (width // 2) + g * (width // 4) + (p % 2) * 128
            return ref[:, pl.ds(pl.multiple_of(start, 128), 128)]

        hid = hidden[...]
        recv, keyv, valv, dirv = [[columns(a, p) for p in P] for a in (rec, key, val, unit)]
        logd = [
            -0.606531 * jax.nn.sigmoid(dot(hid[:, :128], columns(du, p)) + columns(db, p))
            for p in P
        ]
        rate = [jax.nn.sigmoid(dot(hid[:, 128:], columns(ru, p)) + columns(rb, p)) for p in P]
        cum = []
        for p in P:
            l1, l2 = split(logd[p])
            l3 = (logd[p] - l1.astype(F32) - l2.astype(F32)).astype(BF16)
            cum.append(dot(tri2, cat([l1, l2], 0)) + dot(tri, l3))
        mid = [cum[p][T // 2 - 1 : T // 2] for p in P]
        last = [cum[p][T - 1 :] for p in P]
        e_out = [jnp.exp(mid[p] - cum[p]) for p in P]
        dir_in = [dirv[p] * jnp.exp(cum[p] - logd[p] - mid[p]) for p in P]
        read_in = [recv[p].astype(F32) * jnp.exp(cum[p] - mid[p]) for p in P]
        key_out = [keyv[p].astype(F32) * e_out[p] for p in P]
        rem_out = [rate[p] * dirv[p] * e_out[p] for p in P]
        e_mid = [jnp.exp(mid[p]) for p in P]
        e_end = [jnp.exp(last[p] - mid[p]) for p in P]
        e_all = [jnp.exp(last[p]) for p in P]
        scores = []
        zero = jnp.zeros((2 * T, 128), BF16)
        for p in P:
            xh, xl = split(cat([dir_in[p], read_in[p]], 0))
            yh, yl = split(cat([key_out[p], rem_out[p]], 0))
            xr, yr = half_roll(xl), half_roll(yh)
            left = cat([jnp.where(firsts, xh, xr), jnp.where(firsts, xh, zero)], 1)
            scores.append(dot(left, cat([jnp.where(firsts, yh, yr), yl], 1), NT))
            left = cat([jnp.where(firsts, xr, xh), jnp.where(firsts, zero, xh)], 1)
            scores.append(dot(left, cat([jnp.where(firsts, yr, yh), yl], 1), NT))
        a_kk = [jnp.where(strict, scores[h][:T, :T], 0.0) for h in H]
        low = [jnp.where(strict, scores[h][:T, T:], 0.0) for h in H]
        for h in H:
            left_ref[g, h] = cat(
                [
                    jnp.where(upto, -scores[h][T:, T:], 0.0),
                    jnp.where(upto, scores[h][T:, :T], 0.0),
                ],
                1,
            )

        @pl.when(g == 1)
        def _():
            forward(0)

        inv = unit_inverse(low, row, col)
        kv = [dot(cat(split(a_kk[h]), 1), cat([valv[h // 2]] * 2, 0)) for h in H]
        right = [
            cat([dir_in[p] * e_mid[p], jnp.where(first, kv[2 * p], kv[2 * p + 1])], 1) for p in P
        ]
        sol = [mm3(inv[h], right[h // 2]) for h in H]
        low_lane = iota((64, 128), 1) < 64
        for p in P:
            solved = jnp.where(first2, sol[2 * p], sol[2 * p + 1])
            solved_ref[g, p] = solved
            values = cat([jnp.zeros((T, 128), BF16), valv[p]], 1)
            wh, wl = split(solved)
            lh, ll = split(cat([-rem_out[p] * e_end[p], key_out[p] * e_end[p]], 0).T)
            wide = cat([wh, values], 0)
            made = dot(lh, wide) + dot(ll, wide) + dot(lh[:, :T], wl)
            trans = made[:, :128] + eye * e_all[p]
            added = made[:, 128:]
            slot = g * quarter + 2 * (p % 2)
            mu[p // 2, slot] = jnp.where(low_lane, trans[:64], half_roll(added[:64]))
            mu[p // 2, slot + 1] = jnp.where(low_lane, half_roll(trans[64:]), added[64:])
            reff[g, p] = read_in[p] * e_mid[p]
        swap_maps(g).start()
        return carry

    lax.fori_loop(0, 2, half_of_heads, 0)

    def reads_of(i, carry):
        g, p = i // PAIRS, lax.rem(i, PAIRS)
        start = (p // 2) * (width // 2) + g * (width // 4) + lax.rem(p, 2) * 128
        solved = solved_ref[g, p]
        wh, wl = split(solved)
        values = val[:, pl.ds(pl.multiple_of(start, 128), 128)]
        wide = cat([wh, cat([jnp.zeros((T, 128), BF16), values], 1)], 0)
        lh, ll = split(cat([left_ref[g, 2 * p], left_ref[g, 2 * p + 1]], 0))
        made = dot(lh, wide) + dot(ll, wide) + dot(lh[:, :T], wl)
        reads = jnp.where(first2, made[:T], made[T:])
        reff[g, p] = reff[g, p] + reads[:, :128]
        base_ref[g, p] = reads[:, 128:]
        return carry

    lax.fori_loop(0, 3, reads_of, 0)
    forward(1)
    lax.fori_loop(3, 2 * PAIRS, reads_of, 0)

    maps[chip] = chip_maps[my_slot]
    for step in far:
        source = lax.rem(chip + step, chips)
        pltpu.make_async_remote_copy(
            src_ref=chip_maps.at[0],
            dst_ref=maps.at[source],
            send_sem=s1.at[0, 0],
            recv_sem=r1.at[source],
            device_id={"ctx": base + 2 * source + core},
            device_id_type=MESH,
        ).wait_recv()
    prefix = [maps[d] for d in range(chips)]
    size = 1
    while size < chips:
        for low in range(size, chips, 2 * size):
            joined = later_of(cat(prefix[low : low + size], 0), prefix[low - 1])
            for d in range(size):
                prefix[low + d] = joined[64 * d : 64 * d + 64]
        size *= 2
    row_total[...] = prefix[chips - 1]
    second = []
    for step, other in enumerate(rows):
        copy = pltpu.make_async_remote_copy(
            src_ref=row_total,
            dst_ref=row_totals.at[y],
            send_sem=s2.at[step],
            recv_sem=r2.at[step],
            device_id={"ctx": other * n + me},
            device_id_type=MESH,
        )
        copy.start()
        second.append(copy)
    row_totals[y] = row_total[...]
    begin = start_ref[...]
    state = cat([begin, begin], 1)
    for copy in second:
        copy.wait_recv()
    for r in range(nrow - 1):
        state = jnp.where(r < y, later_of(row_totals[r], state), state)
    after_state = later_of(cat(prefix[: chips - 1], 0), state)
    for d in range(chips):
        states[d] = pack_state(state if d == 0 else after_state[64 * d - 64 : 64 * d])
    third = []
    for step, other in enumerate(others):
        copy = pltpu.make_async_remote_copy(
            src_ref=states.at[other],
            dst_ref=got.at[my_slot],
            send_sem=s3.at[step],
            recv_sem=r3.at[step],
            device_id={"ctx": base + 2 * other + core},
            device_id_type=MESH,
        )
        copy.start()
        third.append(copy)
    got[my_slot] = states[chip]
    for copy in third:
        copy.wait_recv()

    for slot in range(chips):
        packed = got[slot]
        full = cat([half_roll(packed), packed], 0)
        next_packed = pack_state(later_of(first_maps[slot], full))
        give[slot] = jnp.where(core == 0, next_packed, packed)
        starts[core, slot] = jnp.where(core == 0, packed, next_packed)
    fourth = pltpu.make_async_remote_copy(
        src_ref=give,
        dst_ref=starts.at[core],
        send_sem=s4.at[0],
        recv_sem=r4.at[0],
        device_id=sibling,
        device_id_type=MESH,
    )
    fourth.start()

    lane = iota((64, 128), 1) < 64
    mean64 = (half.astype(F32) / 64).astype(BF16)
    mean2 = cat([mean64, mean64], 0)

    def finish(side):
        for q in range(chips // 2):
            g, p = q // 2, 2 * side + q % 2
            a, b = starts[side, 2 * q], starts[side, 2 * q + 1]
            both_a = cat([a, half_roll(a)], 0)
            both_b = cat([half_roll(b), b], 0)
            state = cat([jnp.where(lane, both_a, 0.0), jnp.where(lane, 0.0, both_b)], 0)
            read = mm3(reff[g, p], state) + base_ref[g, p]
            centered = read - dot(cat(split(read), 1), mean2)
            var = dot(cat(split(centered * centered), 1), mean2)
            normed = (centered * lax.rsqrt(var + 0.00064)).astype(BF16)
            start = side * (width // 2) + 128 * q
            out[:, pl.ds(pl.multiple_of(start, 128), 128)] = normed

    finish(core)
    fourth.wait()
    finish(other_core)

    for h in range(2):
        swap_maps(h).wait_send()
        for k in range(quarter):
            to, copy = send_map(h, k)

            @pl.when(to != chip)
            def _():
                copy.wait_send()

    for copy in second + third:
        copy.wait_send()


def mixed_of(x, mix, down, du, ru, db, rb, rec, key, val, start, nctx, nhead):
    T, width = x.shape
    n = start.shape[0]
    chips = n // 2
    nrow = nctx // n
    dma, vm = pltpu.SemaphoreType.DMA, pltpu.VMEM
    args = (x, mix, down, du, ru, db, rb, rec, key, val, start)
    return pl.pallas_call(
        functools.partial(mixed_kernel, nctx=nctx, nhead=nhead),
        in_specs=[pl.BlockSpec(memory_space=pl.ANY)] * len(args),
        out_specs=pl.BlockSpec(memory_space=pltpu.VMEM),
        out_shape=pltpu.VMEM((T, width), BF16),
        scratch_shapes=[vm(a.shape, a.dtype) for a in args[:-1]]
        + [vm((64, 64), F32), dma((len(args),))]
        + [
            vm((16, width), BF16),
            vm((T, 256), F32),
            vm((nhead - 1, T // nhead, 256), F32),
            vm((T, 256), BF16),
            dma((2 * nhead,)),
            dma((2 * nhead,)),
            vm((T, width), F32),
            vm((2, chips, 64, 128), F32),
            vm((2, 2 * PAIRS, T, 2 * T), F32),
            vm((2, PAIRS, T, 256), F32),
            vm((2, PAIRS, T, 128), F32),
            vm((2, PAIRS, T, 128), F32),
            vm((2, chips, 32, 128), F32),
            vm((chips, 64, 128), F32),
            vm((chips, 64, 128), F32),
            vm((chips, 64, 128), F32),
            vm((chips, 64, 128), F32),
            vm((64, 128), F32),
            vm((nrow, 64, 128), F32),
            vm((chips, 32, 128), F32),
            vm((chips, 32, 128), F32),
            vm((chips, 32, 128), F32),
        ]
        + [dma((2,)), dma((2,)), dma((2, chips // 2)), dma((chips,)), dma((nrow,)), dma((nrow,))]
        + [dma((chips,)), dma((chips,)), dma((1,)), dma((1,))],
        compiler_params=pltpu.CompilerParams(
            collective_id=0, has_side_effects=True, vmem_limit_bytes=40 * 1024 * 1024
        ),
    )(*[pltpu.with_memory_space_constraint(a, pltpu.HBM) for a in args])


def solution(mesh):
    nctx, nhead = mesh.shape["ctx"], mesh.shape["head"]

    def on_device(x, mix, down, du, ru, db, rb, rec, key, val, start):
        return mixed_of(
            x, mix[None], down, du, ru, db[None], rb[None], rec, key, val, start, nctx, nhead
        )

    P = jax.sharding.PartitionSpec
    both, wide = P("ctx", "head"), P("head")
    return jax.shard_map(
        on_device,
        mesh=mesh,
        in_specs=(both, wide, P("head", None), P(None, "head"), P(None, "head"), wide, wide)
        + (both,) * 3
        + (P("head", None, None),),
        out_specs=both,
        check_vma=False,
    )
```

time: 803 us -> 51.3 us (0.06)
  the two profiles are of different devices: /device:TPU:25 before, /device:TPU:1 now
where the time goes in v2:
time: 51.3 us
  Pallas kernels  50.5 us (98%)
  local copies, waits for them, and re-layouts  0.71 us (1%)
    pallas_call x1, Pallas kernels, mixed_of(): pl.pallas_call(functools.partial(mixed_kernel, nctx=nctx, nhead=nhead), i...  50.5 us

profile of v2, /device:TPU:1, one launch (start us, length us, event | category | flops | bytes accessed | tf_op | source)
XLA Modules:
  0.0 51.3 jit_solution(834586264874760568)
XLA Ops:
  0.0 50.5 %shard_map.109 = bf16[128,1024]{1,0:T(8,128)(2,1)S(1)} custom-call(bf16[128,1024]{1,0:T(8,128)(2,1)} %x_h.1, f32[1,1024]{1,0:T(1,128)} %bitcast.3, bf16[1024,256]{1,0:T(8,128)(2,1)} %down_h.1, bf16[128,1024]{1,0:T(8,128)(2,1)} %du_h.1, bf16[128,1024]{1,0:T(8,128)(2,1)} %ru_h.1, f32[1,1024]{1,0:T(1,128)} %bitcast.4, f32[1,1024]{1,0:T(1,128)} %bitcast.5, ...), custom_call_target="tpu_custom_call" | custom-call | tf_op jit(solution)/shard_map/pallas_call | solution.py:469
  50.6 0.7 %copy.13 = bf16[128,1024]{1,0:T(8,128)(2,1)} copy(bf16[128,1024]{1,0:T(8,128)(2,1)S(1)} %shard_map.109) | data formatting | bytes 524288

commit v3 on v2

--- a/solution.py
+++ b/solution.py
@@ -42,10 +42,17 @@
     return pltpu.roll(x, 64, 1)
 
 
+def later_all(laters, earliers):
+    left = [split(a) for a in laters]
+    right = [[cat([part, jnp.zeros_like(part)], 0) for part in split(b)] for b in earliers]
+    main = [dot(cat([a, al], 1), cat([b, b], 0)) for (a, al), (b, _) in zip(left, right)]
+    rest = [dot(a, bl) for (a, _), (_, bl) in zip(left, right)]
+    lane = [iota(a.shape, 1) < 64 for a in laters]
+    return [m + r + jnp.where(k, 0.0, a) for m, r, k, a in zip(main, rest, lane, laters)]
+
+
 def later_of(map_later, earlier):
-    wide = cat([earlier, jnp.zeros_like(earlier)], 0)
-    lane = iota(map_later.shape, 1) < 64
-    return mm3(map_later, wide) + jnp.where(lane, 0.0, map_later)
+    return later_all([map_later], [earlier])[0]
 
 
 def pack_state(full):
@@ -92,7 +99,8 @@
     out,
     x_ref, mix_ref, down_ref, du, ru, db, rb, rec, key, val, start_ref, loads,
     tail, total, shares, hidden, sends, recvs,
-    unit, mu, left_ref, solved_ref, reff, base_ref, starts,
+    edge_sum, edge_sums, grand_ref, edge_send, edge_recv,
+    unit, mu, cent, outer, solved_ref, reff, base_ref, starts,
     sib, first_maps, chip_maps, maps, row_total, row_totals, states, got, give,
     s0, r0, s1, r1, s2, r2, s3, r3, s4, r4,
     *, nctx, nhead,
@@ -120,10 +128,12 @@
         copy.start()
         fetch.append(copy)
 
+    row_totals[...] = jnp.zeros_like(row_totals)
     after, behind = lax.rem(ctx + 1, nctx), lax.rem(ctx + nctx - 1, nctx)
-    mates = [lax.rem(head + step, nhead) for step in range(1, nhead)]
+    mirror = 1 - 2 * core
+    mates = [lax.rem(head + nhead + mirror * step, nhead) for step in (2, 1, 3)]
     far = sorted(range(1, chips), key=lambda d: -min(d, chips - d))
-    others = [lax.rem(chip + step, chips) for step in far]
+    others = [lax.rem(chip + chips + mirror * step, chips) for step in far]
     rows = [lax.rem(y + step, nrow) for step in range(1, nrow)]
     barrier = pltpu.get_barrier_semaphore()
     for other in [after, behind]:
@@ -151,13 +161,6 @@
     before = pltpu.roll(xf, 1, 0)
     shifted = (xf + (before - xf) * mix).astype(BF16)
     total[...] = dot(shifted, down_ref[...])
-    shift.wait_recv()
-    xt = x_ref[0:16, :].astype(F32)
-    edge = jnp.where(ctx > 0, tail[...].astype(F32)[15:16], 0.0)
-    before = jnp.where(iota((16, width), 0) == 0, edge, pltpu.roll(xt, 1, 0))
-    shifted = (xt + (before - xt) * mix).astype(BF16)
-    total[0:16, :] = dot(shifted, down_ref[...])
-
     share = T // nhead
     mine = pl.ds(pl.multiple_of(head * share, share), share)
     scatter, spread = [], []
@@ -173,6 +176,25 @@
         copy.start()
         scatter.append(copy)
 
+    shift.wait_recv()
+    xt = x_ref[0:16, :].astype(F32)
+    edge = jnp.where(ctx > 0, tail[...].astype(F32)[15:16], 0.0)
+    before = jnp.where(iota((16, width), 0) == 0, edge, pltpu.roll(xt, 1, 0))
+    shifted = (xt + (before - xt) * mix).astype(BF16)
+    edge_sum[...] = dot(shifted, down_ref[...])
+    send_edge = pltpu.make_async_remote_copy(
+        src_ref=edge_sum,
+        dst_ref=edge_sums.at[head],
+        send_sem=edge_send.at[0],
+        recv_sem=edge_recv.at[head],
+        device_id={"head": 0},
+        device_id_type=MESH,
+    )
+
+    @pl.when(head != 0)
+    def _():
+        send_edge.start()
+
     row, col = iota((T, T), 0), iota((T, T), 1)
     tri = (row >= col).astype(BF16)
     half = (row // 64 == col // 64).astype(BF16)
@@ -187,6 +209,24 @@
     for step, copy in enumerate(scatter):
         copy.wait_recv()
         grand = grand + shares[step]
+    grand_ref[...] = grand
+
+    @pl.when(head == 0)
+    def _():
+        first_row = edge_sum[0:1, :]
+        for h in range(1, nhead):
+            pltpu.make_async_remote_copy(
+                src_ref=edge_sum,
+                dst_ref=edge_sums.at[h],
+                send_sem=edge_send.at[0],
+                recv_sem=edge_recv.at[h],
+                device_id={"head": h},
+                device_id_type=MESH,
+            ).wait_recv()
+            first_row = first_row + edge_sums[h, 0:1, :]
+        grand_ref[0:1, :] = first_row
+
+    grand = grand_ref[...]
     hidden[mine, :] = cat([jnp.tanh(grand[:, :128]), grand[:, 128:]], 1).astype(BF16)
     for step, mate in enumerate(mates):
         copy = pltpu.make_async_remote_copy(
@@ -201,11 +241,8 @@
         spread.append(copy)
     for i in range(4, len(fetch)):
         fetch[i].wait()
-    shift.wait_send()
-    for copy in scatter:
-        copy.wait_send()
     for copy in spread:
-        copy.wait()
+        copy.wait_recv()
 
     eye = (row == col).astype(F32)
     first = iota((T, 128), 1) < 64
@@ -227,7 +264,7 @@
         )
 
     def send_map(h, k):
-        place = lax.rem(chip // 2 + k, quarter)
+        place = lax.rem(chip // 2 + quarter + mirror * k, quarter)
         to = 2 * place + h
         return to, pltpu.make_async_remote_copy(
             src_ref=chip_maps.at[h * quarter + place],
@@ -240,19 +277,31 @@
 
     def forward(h):
         swap_maps(h).wait_recv()
-        for i in range(quarter):
-            slot = h * quarter + i
-            own, theirs = mu[core, slot], sib[slot]
-            earlier = jnp.where(core == 0, own, theirs)
-            later = jnp.where(core == 0, theirs, own)
-            first_maps[slot] = earlier
-            chip_maps[slot] = later_of(later, earlier)
+        slots = [h * quarter + i for i in range(quarter)]
+        own, theirs = [mu[core, i] for i in slots], [sib[i] for i in slots]
+        earlier = [jnp.where(core == 0, a, b) for a, b in zip(own, theirs)]
+        later = [jnp.where(core == 0, b, a) for a, b in zip(own, theirs)]
+        joined = later_all(later, earlier)
+        for i, slot in enumerate(slots):
+            chip_maps[slot] = joined[i]
+            first_maps[slot] = earlier[i]
         for k in [2, 1, 3, 0]:
             to, copy = send_map(h, k)
 
             @pl.when(to != chip)
             def _():
                 copy.start()
+
+    def masked_scores(x, yh, yl):
+        xh, xl = split(x)
+        xr, yr = half_roll(xl), half_roll(yh)
+        zero = jnp.zeros_like(xh)
+        a = cat([jnp.where(first, xh, xr), jnp.where(first, xh, zero)], 1)
+        b = cat([jnp.where(first, xr, xh), jnp.where(first, zero, xh)], 1)
+        return [
+            dot(a, cat([jnp.where(firsts, yh, yr), yl], 1), NT),
+            dot(b, cat([jnp.where(firsts, yr, yh), yl], 1), NT),
+        ]
 
     def half_of_heads(g, carry):
         def columns(ref, p):
@@ -282,25 +331,10 @@
         e_end = [jnp.exp(last[p] - mid[p]) for p in P]
         e_all = [jnp.exp(last[p]) for p in P]
         scores = []
-        zero = jnp.zeros((2 * T, 128), BF16)
         for p in P:
-            xh, xl = split(cat([dir_in[p], read_in[p]], 0))
-            yh, yl = split(cat([key_out[p], rem_out[p]], 0))
-            xr, yr = half_roll(xl), half_roll(yh)
-            left = cat([jnp.where(firsts, xh, xr), jnp.where(firsts, xh, zero)], 1)
-            scores.append(dot(left, cat([jnp.where(firsts, yh, yr), yl], 1), NT))
-            left = cat([jnp.where(firsts, xr, xh), jnp.where(firsts, zero, xh)], 1)
-            scores.append(dot(left, cat([jnp.where(firsts, yr, yh), yl], 1), NT))
-        a_kk = [jnp.where(strict, scores[h][:T, :T], 0.0) for h in H]
-        low = [jnp.where(strict, scores[h][:T, T:], 0.0) for h in H]
-        for h in H:
-            left_ref[g, h] = cat(
-                [
-                    jnp.where(upto, -scores[h][T:, T:], 0.0),
-                    jnp.where(upto, scores[h][T:, :T], 0.0),
-                ],
-                1,
-            )
+            scores += masked_scores(dir_in[p], *split(cat([key_out[p], rem_out[p]], 0)))
+        a_kk = [jnp.where(strict, scores[h][:, :T], 0.0) for h in H]
+        low = [jnp.where(strict, scores[h][:, T:], 0.0) for h in H]
 
         @pl.when(g == 1)
         def _():
@@ -313,42 +347,67 @@
         ]
         sol = [mm3(inv[h], right[h // 2]) for h in H]
         low_lane = iota((64, 128), 1) < 64
+        solved = [jnp.where(first2, sol[2 * p], sol[2 * p + 1]) for p in P]
+        ends = [split(cat([-rem_out[p] * e_end[p], key_out[p] * e_end[p]], 0).T) for p in P]
+        made = []
         for p in P:
-            solved = jnp.where(first2, sol[2 * p], sol[2 * p + 1])
-            solved_ref[g, p] = solved
-            values = cat([jnp.zeros((T, 128), BF16), valv[p]], 1)
-            wh, wl = split(solved)
-            lh, ll = split(cat([-rem_out[p] * e_end[p], key_out[p] * e_end[p]], 0).T)
-            wide = cat([wh, values], 0)
-            made = dot(lh, wide) + dot(ll, wide) + dot(lh[:, :T], wl)
-            trans = made[:, :128] + eye * e_all[p]
-            added = made[:, 128:]
+            wh, wl = split(solved[p])
+            lh, ll = ends[p]
+            wide = cat([wh, cat([jnp.zeros((T, 128), BF16), valv[p]], 1)], 0)
+            made.append(dot(lh, wide) + dot(ll, wide) + dot(lh[:, :T], wl))
+        trans = [made[p][:, :128] + eye * e_all[p] for p in P]
+        added = [made[p][:, 128:] for p in P]
+        for p in P:
             slot = g * quarter + 2 * (p % 2)
-            mu[p // 2, slot] = jnp.where(low_lane, trans[:64], half_roll(added[:64]))
-            mu[p // 2, slot + 1] = jnp.where(low_lane, half_roll(trans[64:]), added[64:])
+            mu[p // 2, slot] = jnp.where(low_lane, trans[p][:64], half_roll(added[p][:64]))
+            mu[p // 2, slot + 1] = jnp.where(low_lane, half_roll(trans[p][64:]), added[p][64:])
+        swap_maps(g).start()
+        for p in P:
+            solved_ref[g, p] = solved[p]
             reff[g, p] = read_in[p] * e_mid[p]
-        swap_maps(g).start()
+            cent[g, p] = read_in[p]
+            outer[g, p] = cat([key_out[p], rem_out[p]], 0)
         return carry
 
     lax.fori_loop(0, 2, half_of_heads, 0)
 
     def reads_of(i, carry):
-        g, p = i // PAIRS, lax.rem(i, PAIRS)
-        start = (p // 2) * (width // 2) + g * (width // 4) + lax.rem(p, 2) * 128
-        solved = solved_ref[g, p]
-        wh, wl = split(solved)
-        values = val[:, pl.ds(pl.multiple_of(start, 128), 128)]
-        wide = cat([wh, cat([jnp.zeros((T, 128), BF16), values], 1)], 0)
-        lh, ll = split(cat([left_ref[g, 2 * p], left_ref[g, 2 * p + 1]], 0))
-        made = dot(lh, wide) + dot(ll, wide) + dot(lh[:, :T], wl)
-        reads = jnp.where(first2, made[:T], made[T:])
-        reff[g, p] = reff[g, p] + reads[:, :128]
-        base_ref[g, p] = reads[:, 128:]
+        g, side = i // 2, lax.rem(i, 2)
+        pairs = [2 * side, 2 * side + 1]
+        start = side * (width // 2) + g * (width // 4)
+        values = val[:, pl.ds(pl.multiple_of(start, 256), 256)]
+        solved = [solved_ref[g, p] for p in pairs]
+        inner = [(cent[g, p], outer[g, p]) for p in pairs]
+        before = [reff[g, p] for p in pairs]
+        scores = [masked_scores(x, *split(o)) for x, o in inner]
+        left = [
+            split(
+                cat(
+                    [
+                        cat([jnp.where(upto, -a[:, T:], 0.0), jnp.where(upto, a[:, :T], 0.0)], 1)
+                        for a in both
+                    ],
+                    0,
+                )
+            )
+            for both in scores
+        ]
+        made = []
+        for k in range(2):
+            wh, wl = split(solved[k])
+            zero = jnp.zeros((T, 128), BF16)
+            wide = cat([wh, cat([zero, values[:, 128 * k : 128 * k + 128]], 1)], 0)
+            lh, ll = left[k]
+            made.append(dot(lh, wide) + dot(ll, wide) + dot(lh[:, :T], wl))
+        reads = [jnp.where(first2, a[:T], a[T:]) for a in made]
+        for k in range(2):
+            reff[g, pairs[k]] = before[k] + reads[k][:, :128]
+            base_ref[g, pairs[k]] = reads[k][:, 128:]
         return carry
 
-    lax.fori_loop(0, 3, reads_of, 0)
+    reads_of(0, 0)
     forward(1)
-    lax.fori_loop(3, 2 * PAIRS, reads_of, 0)
+    lax.fori_loop(1, 4, reads_of, 0)
 
     maps[chip] = chip_maps[my_slot]
     for step in far:
@@ -364,34 +423,58 @@
     prefix = [maps[d] for d in range(chips)]
     size = 1
     while size < chips:
-        for low in range(size, chips, 2 * size):
-            joined = later_of(cat(prefix[low : low + size], 0), prefix[low - 1])
+        lows = list(range(size, chips, 2 * size))
+        joined = later_all(
+            [cat(prefix[low : low + size], 0) for low in lows], [prefix[low - 1] for low in lows]
+        )
+        for low, group in zip(lows, joined):
             for d in range(size):
-                prefix[low + d] = joined[64 * d : 64 * d + 64]
+                prefix[low + d] = group[64 * d : 64 * d + 64]
         size *= 2
     row_total[...] = prefix[chips - 1]
-    second = []
-    for step, other in enumerate(rows):
-        copy = pltpu.make_async_remote_copy(
+
+    def send_total(r):
+        return pltpu.make_async_remote_copy(
             src_ref=row_total,
             dst_ref=row_totals.at[y],
-            send_sem=s2.at[step],
-            recv_sem=r2.at[step],
-            device_id={"ctx": other * n + me},
+            send_sem=s2.at[r],
+            recv_sem=r2.at[y],
+            device_id={"ctx": r * n + me},
             device_id_type=MESH,
         )
-        copy.start()
-        second.append(copy)
-    row_totals[y] = row_total[...]
+
+    for r in range(1, nrow):
+
+        @pl.when(r > y)
+        def _():
+            send_total(r).start()
+
     begin = start_ref[...]
     state = cat([begin, begin], 1)
-    for copy in second:
-        copy.wait_recv()
     for r in range(nrow - 1):
-        state = jnp.where(r < y, later_of(row_totals[r], state), state)
+
+        @pl.when(r < y)
+        def _():
+            pltpu.make_async_remote_copy(
+                src_ref=row_total,
+                dst_ref=row_totals.at[r],
+                send_sem=s2.at[r],
+                recv_sem=r2.at[r],
+                device_id={"ctx": r * n + me},
+                device_id_type=MESH,
+            ).wait_recv()
+
+    after_first, others_map = later_all(
+        [row_totals[0], row_totals[2]], [state, row_totals[1]]
+    )
+    others_map = jnp.where(y == 3, others_map, row_totals[1])
+    after_rows = later_of(others_map, after_first)
+    state = jnp.where(y == 0, state, jnp.where(y == 1, after_first, after_rows))
     after_state = later_of(cat(prefix[: chips - 1], 0), state)
+    packs = [pack_state(state)]
+    packs += [pack_state(after_state[64 * d - 64 : 64 * d]) for d in range(1, chips)]
     for d in range(chips):
-        states[d] = pack_state(state if d == 0 else after_state[64 * d - 64 : 64 * d])
+        states[d] = packs[d]
     third = []
     for step, other in enumerate(others):
         copy = pltpu.make_async_remote_copy(
@@ -408,12 +491,14 @@
     for copy in third:
         copy.wait_recv()
 
+    packed = [got[slot] for slot in range(chips)]
+    full = [cat([half_roll(a), a], 0) for a in packed]
+    moved = later_all([first_maps[slot] for slot in range(chips)], full)
+    next_packed = [pack_state(a) for a in moved]
     for slot in range(chips):
-        packed = got[slot]
-        full = cat([half_roll(packed), packed], 0)
-        next_packed = pack_state(later_of(first_maps[slot], full))
-        give[slot] = jnp.where(core == 0, next_packed, packed)
-        starts[core, slot] = jnp.where(core == 0, packed, next_packed)
+        give[slot] = jnp.where(core == 0, next_packed[slot], packed[slot])
+    for slot in range(chips):
+        starts[core, slot] = jnp.where(core == 0, packed[slot], next_packed[slot])
     fourth = pltpu.make_async_remote_copy(
         src_ref=give,
         dst_ref=starts.at[core],
@@ -429,21 +514,26 @@
     mean2 = cat([mean64, mean64], 0)
 
     def finish(side):
-        for q in range(chips // 2):
-            g, p = q // 2, 2 * side + q % 2
+        Q = range(chips // 2)
+        state = []
+        for q in Q:
             a, b = starts[side, 2 * q], starts[side, 2 * q + 1]
             both_a = cat([a, half_roll(a)], 0)
             both_b = cat([half_roll(b), b], 0)
-            state = cat([jnp.where(lane, both_a, 0.0), jnp.where(lane, 0.0, both_b)], 0)
-            read = mm3(reff[g, p], state) + base_ref[g, p]
-            centered = read - dot(cat(split(read), 1), mean2)
-            var = dot(cat(split(centered * centered), 1), mean2)
-            normed = (centered * lax.rsqrt(var + 0.00064)).astype(BF16)
+            state.append(
+                cat([jnp.where(lane, both_a, 0.0), jnp.where(lane, 0.0, both_b)], 0)
+            )
+        place = [(q // 2, 2 * side + q % 2) for q in Q]
+        read = [mm3(reff[place[q]], state[q]) + base_ref[place[q]] for q in Q]
+        centered = [a - dot(cat(split(a), 1), mean2) for a in read]
+        var = [dot(cat(split(a * a), 1), mean2) for a in centered]
+        normed = [(a * lax.rsqrt(b + 0.00064)).astype(BF16) for a, b in zip(centered, var)]
+        for q in Q:
             start = side * (width // 2) + 128 * q
-            out[:, pl.ds(pl.multiple_of(start, 128), 128)] = normed
+            out[:, pl.ds(pl.multiple_of(start, 128), 128)] = normed[q]
 
     finish(core)
-    fourth.wait()
+    fourth.wait_recv()
     finish(other_core)
 
     for h in range(2):
@@ -455,8 +545,18 @@
             def _():
                 copy.wait_send()
 
-    for copy in second + third:
+    for r in range(1, nrow):
+
+        @pl.when(r > y)
+        def _():
+            send_total(r).wait_send()
+
+    for copy in [shift, fourth] + scatter + spread + third:
         copy.wait_send()
+
+    @pl.when(head != 0)
+    def _():
+        send_edge.wait_send()
 
 
 def mixed_of(x, mix, down, du, ru, db, rb, rec, key, val, start, nctx, nhead):
@@ -480,9 +580,15 @@
             vm((T, 256), BF16),
             dma((2 * nhead,)),
             dma((2 * nhead,)),
+            vm((16, 256), F32),
+            vm((nhead, 16, 256), F32),
+            vm((T // nhead, 256), F32),
+            dma((1,)),
+            dma((nhead,)),
             vm((T, width), F32),
             vm((2, chips, 64, 128), F32),
-            vm((2, 2 * PAIRS, T, 2 * T), F32),
+            vm((2, PAIRS, T, 128), F32),
+            vm((2, PAIRS, 2 * T, 128), F32),
             vm((2, PAIRS, T, 256), F32),
             vm((2, PAIRS, T, 128), F32),
             vm((2, PAIRS, T, 128), F32),

time: 51.3 us -> 46.9 us (0.914)
  the two profiles are of different devices: /device:TPU:1 before, /device:TPU:27 now
where the time goes in v3:
time: 46.9 us; the launch traced here: 46.8 us
  Pallas kernels  46.1 us (98%)
  local copies, waits for them, and re-layouts  0.71 us (2%)
    pallas_call x1, Pallas kernels, mixed_of(): pl.pallas_call(functools.partial(mixed_kernel, nctx=nctx, nhead=nhead), i...  46.1 us

profile of v3, /device:TPU:27, one launch (start us, length us, event | category | flops | bytes accessed | tf_op | source)
XLA Modules:
  0.0 46.8 jit_solution(14942500277694772259)
XLA Ops:
  0.0 46.1 %shard_map.109 = bf16[128,1024]{1,0:T(8,128)(2,1)S(1)} custom-call(bf16[128,1024]{1,0:T(8,128)(2,1)} %x_h.1, f32[1,1024]{1,0:T(1,128)} %bitcast.3, bf16[1024,256]{1,0:T(8,128)(2,1)} %down_h.1, bf16[128,1024]{1,0:T(8,128)(2,1)} %du_h.1, bf16[128,1024]{1,0:T(8,128)(2,1)} %ru_h.1, f32[1,1024]{1,0:T(1,128)} %bitcast.4, f32[1,1024]{1,0:T(1,128)} %bitcast.5, ...), custom_call_target="tpu_custom_call" | custom-call | tf_op jit(solution)/shard_map/pallas_call | solution.py:569
  46.1 0.7 %copy.13 = bf16[128,1024]{1,0:T(8,128)(2,1)} copy(bf16[128,1024]{1,0:T(8,128)(2,1)S(1)} %shard_map.109) | data formatting | bytes 524288

commit v4 on v3

--- a/solution.py
+++ b/solution.py
@@ -99,7 +99,7 @@
     out,
     x_ref, mix_ref, down_ref, du, ru, db, rb, rec, key, val, start_ref, loads,
     tail, total, shares, hidden, sends, recvs,
-    edge_sum, edge_sums, grand_ref, edge_send, edge_recv,
+    edge_sum, edge_sums, ready, edge_send, edge_recv,
     unit, mu, cent, outer, solved_ref, reff, base_ref, starts,
     sib, first_maps, chip_maps, maps, row_total, row_totals, states, got, give,
     s0, r0, s1, r1, s2, r2, s3, r3, s4, r4,
@@ -124,9 +124,9 @@
         [(x_h, x_ref), (mix_h, mix_ref), (down_h, down_ref), (key_h, key), (du_h, du), (ru_h, ru)]
         + [(db_h, db), (rb_h, rb), (rec_h, rec), (val_h, val), (start_h.at[my_head], start_ref)]
     ):
-        copy = pltpu.make_async_copy(src, dst, loads.at[i])
+        fetch.append(pltpu.make_async_copy(src, dst, loads.at[i]))
+    for copy in fetch[:4]:
         copy.start()
-        fetch.append(copy)
 
     row_totals[...] = jnp.zeros_like(row_totals)
     after, behind = lax.rem(ctx + 1, nctx), lax.rem(ctx + nctx - 1, nctx)
@@ -143,6 +143,16 @@
     pl.semaphore_signal(barrier, inc=1, device_id=sibling, device_id_type=MESH)
     for other in [base + 2 * o + core for o in others] + [r * n + me for r in rows]:
         pl.semaphore_signal(barrier, inc=1, device_id={"ctx": other}, device_id_type=MESH)
+
+    for i in range(3):
+        fetch[i].wait()
+    for copy in fetch[4:]:
+        copy.start()
+    mix = mix_ref[...]
+    xf = x_ref[...].astype(F32)
+    before = pltpu.roll(xf, 1, 0)
+    shifted = (xf + (before - xf) * mix).astype(BF16)
+    total[...] = dot(shifted, down_ref[...])
     pl.semaphore_wait(barrier, 2 + nhead - 1 + 1 + chips - 1 + nrow - 1)
 
     shift = pltpu.make_async_remote_copy(
@@ -154,13 +164,7 @@
         device_id_type=MESH,
     )
     shift.start()
-    for i in range(3):
-        fetch[i].wait()
-    mix = mix_ref[...]
-    xf = x_ref[...].astype(F32)
-    before = pltpu.roll(xf, 1, 0)
-    shifted = (xf + (before - xf) * mix).astype(BF16)
-    total[...] = dot(shifted, down_ref[...])
+
     share = T // nhead
     mine = pl.ds(pl.multiple_of(head * share, share), share)
     scatter, spread = [], []
@@ -182,18 +186,18 @@
     before = jnp.where(iota((16, width), 0) == 0, edge, pltpu.roll(xt, 1, 0))
     shifted = (xt + (before - xt) * mix).astype(BF16)
     edge_sum[...] = dot(shifted, down_ref[...])
-    send_edge = pltpu.make_async_remote_copy(
-        src_ref=edge_sum,
-        dst_ref=edge_sums.at[head],
-        send_sem=edge_send.at[0],
-        recv_sem=edge_recv.at[head],
-        device_id={"head": 0},
-        device_id_type=MESH,
-    )
-
-    @pl.when(head != 0)
-    def _():
-        send_edge.start()
+    edges = []
+    for step, mate in enumerate(mates):
+        copy = pltpu.make_async_remote_copy(
+            src_ref=edge_sum,
+            dst_ref=edge_sums.at[step],
+            send_sem=edge_send.at[step],
+            recv_sem=edge_recv.at[step],
+            device_id={"head": mate},
+            device_id_type=MESH,
+        )
+        copy.start()
+        edges.append(copy)
 
     row, col = iota((T, T), 0), iota((T, T), 1)
     tri = (row >= col).astype(BF16)
@@ -209,24 +213,6 @@
     for step, copy in enumerate(scatter):
         copy.wait_recv()
         grand = grand + shares[step]
-    grand_ref[...] = grand
-
-    @pl.when(head == 0)
-    def _():
-        first_row = edge_sum[0:1, :]
-        for h in range(1, nhead):
-            pltpu.make_async_remote_copy(
-                src_ref=edge_sum,
-                dst_ref=edge_sums.at[h],
-                send_sem=edge_send.at[0],
-                recv_sem=edge_recv.at[h],
-                device_id={"head": h},
-                device_id_type=MESH,
-            ).wait_recv()
-            first_row = first_row + edge_sums[h, 0:1, :]
-        grand_ref[0:1, :] = first_row
-
-    grand = grand_ref[...]
     hidden[mine, :] = cat([jnp.tanh(grand[:, :128]), grand[:, 128:]], 1).astype(BF16)
     for step, mate in enumerate(mates):
         copy = pltpu.make_async_remote_copy(
@@ -241,8 +227,16 @@
         spread.append(copy)
     for i in range(4, len(fetch)):
         fetch[i].wait()
+    first_row = edge_sum[0:8, :]
+    for step, copy in enumerate(edges):
+        copy.wait_recv()
+        first_row = first_row + edge_sums[step, 0:8, :]
+    first_row = cat([jnp.tanh(first_row[:1, :128]), first_row[:1, 128:]], 1)
     for copy in spread:
         copy.wait_recv()
+    ready[...] = jnp.where(
+        iota((T, 256), 0) == 0, first_row, hidden[...].astype(F32)
+    ).astype(BF16)
 
     eye = (row == col).astype(F32)
     first = iota((T, 128), 1) < 64
@@ -308,7 +302,7 @@
             start = (p // 2) * (width // 2) + g * (width // 4) + (p % 2) * 128
             return ref[:, pl.ds(pl.multiple_of(start, 128), 128)]
 
-        hid = hidden[...]
+        hid = ready[...]
         recv, keyv, valv, dirv = [[columns(a, p) for p in P] for a in (rec, key, val, unit)]
         logd = [
             -0.606531 * jax.nn.sigmoid(dot(hid[:, :128], columns(du, p)) + columns(db, p))
@@ -481,60 +475,78 @@
             src_ref=states.at[other],
             dst_ref=got.at[my_slot],
             send_sem=s3.at[step],
-            recv_sem=r3.at[step],
+            recv_sem=r3.at[my_slot],
             device_id={"ctx": base + 2 * other + core},
             device_id_type=MESH,
         )
         copy.start()
         third.append(copy)
     got[my_slot] = states[chip]
-    for copy in third:
-        copy.wait_recv()
-
-    packed = [got[slot] for slot in range(chips)]
-    full = [cat([half_roll(a), a], 0) for a in packed]
-    moved = later_all([first_maps[slot] for slot in range(chips)], full)
-    next_packed = [pack_state(a) for a in moved]
-    for slot in range(chips):
-        give[slot] = jnp.where(core == 0, next_packed[slot], packed[slot])
-    for slot in range(chips):
-        starts[core, slot] = jnp.where(core == 0, packed[slot], next_packed[slot])
-    fourth = pltpu.make_async_remote_copy(
-        src_ref=give,
-        dst_ref=starts.at[core],
-        send_sem=s4.at[0],
-        recv_sem=r4.at[0],
-        device_id=sibling,
-        device_id_type=MESH,
-    )
-    fourth.start()
+
+    def swap_states(h):
+        part = pl.ds(h * quarter, quarter)
+        return pltpu.make_async_remote_copy(
+            src_ref=give.at[part],
+            dst_ref=starts.at[core, part],
+            send_sem=s4.at[h],
+            recv_sem=r4.at[h],
+            device_id=sibling,
+            device_id_type=MESH,
+        )
+
+    def take(h):
+        slots = range(h * quarter, h * quarter + quarter)
+        for slot in slots:
+
+            @pl.when(slot != my_slot)
+            def _():
+                pltpu.make_async_remote_copy(
+                    src_ref=states.at[0],
+                    dst_ref=got.at[slot],
+                    send_sem=s3.at[0],
+                    recv_sem=r3.at[slot],
+                    device_id=sibling,
+                    device_id_type=MESH,
+                ).wait_recv()
+
+        packed = [got[slot] for slot in slots]
+        full = [cat([half_roll(a), a], 0) for a in packed]
+        moved = later_all([first_maps[slot] for slot in slots], full)
+        next_packed = [pack_state(a) for a in moved]
+        for i, slot in enumerate(slots):
+            give[slot] = jnp.where(core == 0, next_packed[i], packed[i])
+        swap_states(h).start()
+        for i, slot in enumerate(slots):
+            starts[core, slot] = jnp.where(core == 0, packed[i], next_packed[i])
 
     lane = iota((64, 128), 1) < 64
     mean64 = (half.astype(F32) / 64).astype(BF16)
     mean2 = cat([mean64, mean64], 0)
 
-    def finish(side):
-        Q = range(chips // 2)
+    def finish(side, h):
+        Q = range(2)
         state = []
         for q in Q:
-            a, b = starts[side, 2 * q], starts[side, 2 * q + 1]
+            a, b = [starts[side, h * quarter + 2 * q + k] for k in range(2)]
             both_a = cat([a, half_roll(a)], 0)
             both_b = cat([half_roll(b), b], 0)
             state.append(
                 cat([jnp.where(lane, both_a, 0.0), jnp.where(lane, 0.0, both_b)], 0)
             )
-        place = [(q // 2, 2 * side + q % 2) for q in Q]
+        place = [(h, 2 * side + q) for q in Q]
         read = [mm3(reff[place[q]], state[q]) + base_ref[place[q]] for q in Q]
         centered = [a - dot(cat(split(a), 1), mean2) for a in read]
         var = [dot(cat(split(a * a), 1), mean2) for a in centered]
         normed = [(a * lax.rsqrt(b + 0.00064)).astype(BF16) for a, b in zip(centered, var)]
         for q in Q:
-            start = side * (width // 2) + 128 * q
+            start = side * (width // 2) + h * (width // 4) + 128 * q
             out[:, pl.ds(pl.multiple_of(start, 128), 128)] = normed[q]
 
-    finish(core)
-    fourth.wait_recv()
-    finish(other_core)
+    for h in range(2):
+        take(h)
+        finish(core, h)
+        swap_states(h).wait_recv()
+        finish(other_core, h)
 
     for h in range(2):
         swap_maps(h).wait_send()
@@ -551,12 +563,8 @@
         def _():
             send_total(r).wait_send()
 
-    for copy in [shift, fourth] + scatter + spread + third:
+    for copy in [shift, swap_states(0), swap_states(1)] + scatter + edges + spread + third:
         copy.wait_send()
-
-    @pl.when(head != 0)
-    def _():
-        send_edge.wait_send()
 
 
 def mixed_of(x, mix, down, du, ru, db, rb, rec, key, val, start, nctx, nhead):
@@ -581,10 +589,10 @@
             dma((2 * nhead,)),
             dma((2 * nhead,)),
             vm((16, 256), F32),
-            vm((nhead, 16, 256), F32),
-            vm((T // nhead, 256), F32),
-            dma((1,)),
-            dma((nhead,)),
+            vm((nhead - 1, 16, 256), F32),
+            vm((T, 256), BF16),
+            dma((nhead - 1,)),
+            dma((nhead - 1,)),
             vm((T, width), F32),
             vm((2, chips, 64, 128), F32),
             vm((2, PAIRS, T, 128), F32),
@@ -604,7 +612,7 @@
             vm((chips, 32, 128), F32),
         ]
         + [dma((2,)), dma((2,)), dma((2, chips // 2)), dma((chips,)), dma((nrow,)), dma((nrow,))]
-        + [dma((chips,)), dma((chips,)), dma((1,)), dma((1,))],
+        + [dma((chips,)), dma((chips,)), dma((2,)), dma((2,))],
         compiler_params=pltpu.CompilerParams(
             collective_id=0, has_side_effects=True, vmem_limit_bytes=40 * 1024 * 1024
         ),

time: 46.9 us -> 45 us (0.959)
  the two profiles are of different devices: /device:TPU:27 before, /device:TPU:25 now
where the time goes in v4:
time: 45 us; the launch traced here: 44.9 us
  Pallas kernels  44.1 us (98%)
  local copies, waits for them, and re-layouts  0.71 us (2%)
    pallas_call x1, Pallas kernels, mixed_of(): pl.pallas_call(functools.partial(mixed_kernel, nctx=nctx, nhead=nhead), i...  44.1 us

profile of v4, /device:TPU:25, one launch (start us, length us, event | category | flops | bytes accessed | tf_op | source)
XLA Modules:
  0.0 44.9 jit_solution(17773577486946908228)
XLA Ops:
  0.0 44.1 %shard_map.109 = bf16[128,1024]{1,0:T(8,128)(2,1)S(1)} custom-call(bf16[128,1024]{1,0:T(8,128)(2,1)} %x_h.1, f32[1,1024]{1,0:T(1,128)} %bitcast.3, bf16[1024,256]{1,0:T(8,128)(2,1)} %down_h.1, bf16[128,1024]{1,0:T(8,128)(2,1)} %du_h.1, bf16[128,1024]{1,0:T(8,128)(2,1)} %ru_h.1, f32[1,1024]{1,0:T(1,128)} %bitcast.4, f32[1,1024]{1,0:T(1,128)} %bitcast.5, ...), custom_call_target="tpu_custom_call" | custom-call | tf_op jit(solution)/shard_map/pallas_call | solution.py:577
  44.2 0.7 %copy.13 = bf16[128,1024]{1,0:T(8,128)(2,1)} copy(bf16[128,1024]{1,0:T(8,128)(2,1)S(1)} %shard_map.109) | data formatting | bytes 524288

commit v5 on v4

--- a/solution.py
+++ b/solution.py
@@ -125,8 +125,6 @@
         + [(db_h, db), (rb_h, rb), (rec_h, rec), (val_h, val), (start_h.at[my_head], start_ref)]
     ):
         fetch.append(pltpu.make_async_copy(src, dst, loads.at[i]))
-    for copy in fetch[:4]:
-        copy.start()
 
     row_totals[...] = jnp.zeros_like(row_totals)
     after, behind = lax.rem(ctx + 1, nctx), lax.rem(ctx + nctx - 1, nctx)
@@ -136,13 +134,15 @@
     others = [lax.rem(chip + chips + mirror * step, chips) for step in far]
     rows = [lax.rem(y + step, nrow) for step in range(1, nrow)]
     barrier = pltpu.get_barrier_semaphore()
-    for other in [after, behind]:
+    for other in [base + 2 * o + core for o in others] + [r * n + me for r in rows]:
         pl.semaphore_signal(barrier, inc=1, device_id={"ctx": other}, device_id_type=MESH)
     for mate in mates:
         pl.semaphore_signal(barrier, inc=1, device_id={"head": mate}, device_id_type=MESH)
+    for other in [after, behind]:
+        pl.semaphore_signal(barrier, inc=1, device_id={"ctx": other}, device_id_type=MESH)
     pl.semaphore_signal(barrier, inc=1, device_id=sibling, device_id_type=MESH)
-    for other in [base + 2 * o + core for o in others] + [r * n + me for r in rows]:
-        pl.semaphore_signal(barrier, inc=1, device_id={"ctx": other}, device_id_type=MESH)
+    for copy in fetch[:4]:
+        copy.start()
 
     for i in range(3):
         fetch[i].wait()
@@ -153,6 +153,16 @@
     before = pltpu.roll(xf, 1, 0)
     shifted = (xf + (before - xf) * mix).astype(BF16)
     total[...] = dot(shifted, down_ref[...])
+
+    row, col = iota((T, T), 0), iota((T, T), 1)
+    tri = (row >= col).astype(BF16)
+    half = (row // 64 == col // 64).astype(BF16)
+    half2 = cat([half, half], 0)
+    fetch[3].wait()
+    for p in range(width // 128):
+        kf = key[:, 128 * p : 128 * p + 128].astype(F32)
+        square = dot(cat(split(kf * kf), 1), half2)
+        unit[:, 128 * p : 128 * p + 128] = kf * lax.rsqrt(square + 1e-06)
     pl.semaphore_wait(barrier, 2 + nhead - 1 + 1 + chips - 1 + nrow - 1)
 
     shift = pltpu.make_async_remote_copy(
@@ -198,16 +208,6 @@
         )
         copy.start()
         edges.append(copy)
-
-    row, col = iota((T, T), 0), iota((T, T), 1)
-    tri = (row >= col).astype(BF16)
-    half = (row // 64 == col // 64).astype(BF16)
-    half2 = cat([half, half], 0)
-    fetch[3].wait()
-    for p in range(width // 128):
-        kf = key[:, 128 * p : 128 * p + 128].astype(F32)
-        square = dot(cat(split(kf * kf), 1), half2)
-        unit[:, 128 * p : 128 * p + 128] = kf * lax.rsqrt(square + 1e-06)
 
     grand = total[mine, :]
     for step, copy in enumerate(scatter):
@@ -399,9 +399,8 @@
             base_ref[g, pairs[k]] = reads[k][:, 128:]
         return carry
 
-    reads_of(0, 0)
     forward(1)
-    lax.fori_loop(1, 4, reads_of, 0)
+    lax.fori_loop(0, 4, reads_of, 0)
 
     maps[chip] = chip_maps[my_slot]
     for step in far:

time: 45 us -> 44.8 us (level)
  no operation moved by 1% of the time
where the time goes in v5:
time: 44.8 us
  Pallas kernels  44 us (98%)
  local copies, waits for them, and re-layouts  0.71 us (2%)
    pallas_call x1, Pallas kernels, mixed_of(): pl.pallas_call(functools.partial(mixed_kernel, nctx=nctx, nhead=nhead), i...  44 us

profile of v5, /device:TPU:25, one launch (start us, length us, event | category | flops | bytes accessed | tf_op | source)
XLA Modules:
  0.0 44.8 jit_solution(15414732696270441781)
XLA Ops:
  0.0 44.0 %shard_map.109 = bf16[128,1024]{1,0:T(8,128)(2,1)S(1)} custom-call(bf16[128,1024]{1,0:T(8,128)(2,1)} %x_h.1, f32[1,1024]{1,0:T(1,128)} %bitcast.3, bf16[1024,256]{1,0:T(8,128)(2,1)} %down_h.1, bf16[128,1024]{1,0:T(8,128)(2,1)} %du_h.1, bf16[128,1024]{1,0:T(8,128)(2,1)} %ru_h.1, f32[1,1024]{1,0:T(1,128)} %bitcast.4, f32[1,1024]{1,0:T(1,128)} %bitcast.5, ...), custom_call_target="tpu_custom_call" | custom-call | tf_op jit(solution)/shard_map/pallas_call | solution.py:576
  44.1 0.7 %copy.13 = bf16[128,1024]{1,0:T(8,128)(2,1)} copy(bf16[128,1024]{1,0:T(8,128)(2,1)S(1)} %shard_map.109) | data formatting | bytes 524288

commit v6 on v5

--- a/solution.py
+++ b/solution.py
@@ -494,7 +494,7 @@
         )
 
     def take(h):
-        slots = range(h * quarter, h * quarter + quarter)
+        slots = [h * quarter + i for i in range(quarter)]
         for slot in slots:
 
             @pl.when(slot != my_slot)
@@ -541,11 +541,14 @@
             start = side * (width // 2) + h * (width // 4) + 128 * q
             out[:, pl.ds(pl.multiple_of(start, 128), 128)] = normed[q]
 
-    for h in range(2):
+    def settle(h, carry):
         take(h)
         finish(core, h)
         swap_states(h).wait_recv()
         finish(other_core, h)
+        return carry
+
+    lax.fori_loop(0, 2, settle, 0)
 
     for h in range(2):
         swap_maps(h).wait_send()

time: 44.8 us -> 44.8 us (level)
  no operation moved by 1% of the time
where the time goes in v6:
time: 44.8 us; the launch traced here: 44.7 us
  Pallas kernels  44 us (98%)
  local copies, waits for them, and re-layouts  0.71 us (2%)
    pallas_call x1, Pallas kernels, mixed_of(): pl.pallas_call(functools.partial(mixed_kernel, nctx=nctx, nhead=nhead), i...  44 us

profile of v6, /device:TPU:25, one launch (start us, length us, event | category | flops | bytes accessed | tf_op | source)
XLA Modules:
  0.0 44.7 jit_solution(10586396327460910902)
XLA Ops:
  0.0 44.0 %shard_map.109 = bf16[128,1024]{1,0:T(8,128)(2,1)S(1)} custom-call(bf16[128,1024]{1,0:T(8,128)(2,1)} %x_h.1, f32[1,1024]{1,0:T(1,128)} %bitcast.3, bf16[1024,256]{1,0:T(8,128)(2,1)} %down_h.1, bf16[128,1024]{1,0:T(8,128)(2,1)} %du_h.1, bf16[128,1024]{1,0:T(8,128)(2,1)} %ru_h.1, f32[1,1024]{1,0:T(1,128)} %bitcast.4, f32[1,1024]{1,0:T(1,128)} %bitcast.5, ...), custom_call_target="tpu_custom_call" | custom-call | tf_op jit(solution)/shard_map/pallas_call | solution.py:579
  44.0 0.7 %copy.13 = bf16[128,1024]{1,0:T(8,128)(2,1)} copy(bf16[128,1024]{1,0:T(8,128)(2,1)S(1)} %shard_map.109) | data formatting | bytes 524288

commit v7 on v6

--- a/solution.py
+++ b/solution.py
@@ -99,7 +99,7 @@
     out,
     x_ref, mix_ref, down_ref, du, ru, db, rb, rec, key, val, start_ref, loads,
     tail, total, shares, hidden, sends, recvs,
-    edge_sum, edge_sums, ready, edge_send, edge_recv,
+    edge_sum, edge_sums, ready, edge_send, edge_recv, val_high, val_low,
     unit, mu, cent, outer, solved_ref, reff, base_ref, starts,
     sib, first_maps, chip_maps, maps, row_total, row_totals, states, got, give,
     s0, r0, s1, r1, s2, r2, s3, r3, s4, r4,
@@ -199,7 +199,7 @@
     edges = []
     for step, mate in enumerate(mates):
         copy = pltpu.make_async_remote_copy(
-            src_ref=edge_sum,
+            src_ref=edge_sum.at[pl.ds(0, 8)],
             dst_ref=edge_sums.at[step],
             send_sem=edge_send.at[step],
             recv_sem=edge_recv.at[step],
@@ -227,10 +227,17 @@
         spread.append(copy)
     for i in range(4, len(fetch)):
         fetch[i].wait()
+    mean64 = (half.astype(F32) / 64).astype(BF16)
+    for p in range(width // 128):
+        cols = slice(128 * p, 128 * p + 128)
+        values = val[:, cols]
+        vh, vl = split(values.astype(F32) - dot(values, mean64))
+        val_high[:, cols] = vh
+        val_low[:, cols] = vl
     first_row = edge_sum[0:8, :]
     for step, copy in enumerate(edges):
         copy.wait_recv()
-        first_row = first_row + edge_sums[step, 0:8, :]
+        first_row = first_row + edge_sums[step]
     first_row = cat([jnp.tanh(first_row[:1, :128]), first_row[:1, 128:]], 1)
     for copy in spread:
         copy.wait_recv()
@@ -303,7 +310,8 @@
             return ref[:, pl.ds(pl.multiple_of(start, 128), 128)]
 
         hid = ready[...]
-        recv, keyv, valv, dirv = [[columns(a, p) for p in P] for a in (rec, key, val, unit)]
+        recv, keyv, dirv = [[columns(a, p) for p in P] for a in (rec, key, unit)]
+        val_h, val_l = [[columns(a, p) for p in P] for a in (val_high, val_low)]
         logd = [
             -0.606531 * jax.nn.sigmoid(dot(hid[:, :128], columns(du, p)) + columns(db, p))
             for p in P
@@ -335,7 +343,11 @@
             forward(0)
 
         inv = unit_inverse(low, row, col)
-        kv = [dot(cat(split(a_kk[h]), 1), cat([valv[h // 2]] * 2, 0)) for h in H]
+        kk = [split(a) for a in a_kk]
+        kv = [
+            dot(cat(kk[h], 1), cat([val_h[h // 2]] * 2, 0)) + dot(kk[h][0], val_l[h // 2])
+            for h in H
+        ]
         right = [
             cat([dir_in[p] * e_mid[p], jnp.where(first, kv[2 * p], kv[2 * p + 1])], 1) for p in P
         ]
@@ -347,8 +359,10 @@
         for p in P:
             wh, wl = split(solved[p])
             lh, ll = ends[p]
-            wide = cat([wh, cat([jnp.zeros((T, 128), BF16), valv[p]], 1)], 0)
-            made.append(dot(lh, wide) + dot(ll, wide) + dot(lh[:, :T], wl))
+            zero = jnp.zeros((T, 128), BF16)
+            wide = cat([wh, cat([zero, val_h[p]], 1)], 0)
+            rest = cat([wl, cat([zero, val_l[p]], 1)], 0)
+            made.append(dot(lh, wide) + dot(ll, wide) + dot(lh, rest))
         trans = [made[p][:, :128] + eye * e_all[p] for p in P]
         added = [made[p][:, 128:] for p in P]
         for p in P:
@@ -369,7 +383,8 @@
         g, side = i // 2, lax.rem(i, 2)
         pairs = [2 * side, 2 * side + 1]
         start = side * (width // 2) + g * (width // 4)
-        values = val[:, pl.ds(pl.multiple_of(start, 256), 256)]
+        cols = pl.ds(pl.multiple_of(start, 256), 256)
+        high, low_part = val_high[:, cols], val_low[:, cols]
         solved = [solved_ref[g, p] for p in pairs]
         inner = [(cent[g, p], outer[g, p]) for p in pairs]
         before = [reff[g, p] for p in pairs]
@@ -390,9 +405,11 @@
         for k in range(2):
             wh, wl = split(solved[k])
             zero = jnp.zeros((T, 128), BF16)
-            wide = cat([wh, cat([zero, values[:, 128 * k : 128 * k + 128]], 1)], 0)
+            side_cols = slice(128 * k, 128 * k + 128)
+            wide = cat([wh, cat([zero, high[:, side_cols]], 1)], 0)
+            rest = cat([wl, cat([zero, low_part[:, side_cols]], 1)], 0)
             lh, ll = left[k]
-            made.append(dot(lh, wide) + dot(ll, wide) + dot(lh[:, :T], wl))
+            made.append(dot(lh, wide) + dot(ll, wide) + dot(lh, rest))
         reads = [jnp.where(first2, a[:T], a[T:]) for a in made]
         for k in range(2):
             reff[g, pairs[k]] = before[k] + reads[k][:, :128]
@@ -443,6 +460,7 @@
             send_total(r).start()
 
     begin = start_ref[...]
+    begin = begin - jnp.mean(begin, axis=1, keepdims=True)
     state = cat([begin, begin], 1)
     for r in range(nrow - 1):
 
@@ -519,7 +537,6 @@
             starts[core, slot] = jnp.where(core == 0, packed[i], next_packed[i])
 
     lane = iota((64, 128), 1) < 64
-    mean64 = (half.astype(F32) / 64).astype(BF16)
     mean2 = cat([mean64, mean64], 0)
 
     def finish(side, h):
@@ -533,8 +550,7 @@
                 cat([jnp.where(lane, both_a, 0.0), jnp.where(lane, 0.0, both_b)], 0)
             )
         place = [(h, 2 * side + q) for q in Q]
-        read = [mm3(reff[place[q]], state[q]) + base_ref[place[q]] for q in Q]
-        centered = [a - dot(cat(split(a), 1), mean2) for a in read]
+        centered = [mm3(reff[place[q]], state[q]) + base_ref[place[q]] for q in Q]
         var = [dot(cat(split(a * a), 1), mean2) for a in centered]
         normed = [(a * lax.rsqrt(b + 0.00064)).astype(BF16) for a, b in zip(centered, var)]
         for q in Q:
@@ -591,10 +607,12 @@
             dma((2 * nhead,)),
             dma((2 * nhead,)),
             vm((16, 256), F32),
-            vm((nhead - 1, 16, 256), F32),
+            vm((nhead - 1, 8, 256), F32),
             vm((T, 256), BF16),
             dma((nhead - 1,)),
             dma((nhead - 1,)),
+            vm((T, width), BF16),
+            vm((T, width), BF16),
             vm((T, width), F32),
             vm((2, chips, 64, 128), F32),
             vm((2, PAIRS, T, 128), F32),

time: 44.8 us -> 44.8 us (level)
  no operation moved by 1% of the time
where the time goes in v7:
time: 44.8 us; the launch traced here: 44.7 us
  Pallas kernels  44 us (98%)
  local copies, waits for them, and re-layouts  0.71 us (2%)
    pallas_call x1, Pallas kernels, mixed_of(): pl.pallas_call(functools.partial(mixed_kernel, nctx=nctx, nhead=nhead), i...  44 us

profile of v7, /device:TPU:25, one launch (start us, length us, event | category | flops | bytes accessed | tf_op | source)
XLA Modules:
  0.0 44.7 jit_solution(16747108451793028366)
XLA Ops:
  0.0 44.0 %shard_map.109 = bf16[128,1024]{1,0:T(8,128)(2,1)S(1)} custom-call(bf16[128,1024]{1,0:T(8,128)(2,1)} %x_h.1, f32[1,1024]{1,0:T(1,128)} %bitcast.3, bf16[1024,256]{1,0:T(8,128)(2,1)} %down_h.1, bf16[128,1024]{1,0:T(8,128)(2,1)} %du_h.1, bf16[128,1024]{1,0:T(8,128)(2,1)} %ru_h.1, f32[1,1024]{1,0:T(1,128)} %bitcast.4, f32[1,1024]{1,0:T(1,128)} %bitcast.5, ...), custom_call_target="tpu_custom_call" | custom-call | tf_op jit(solution)/shard_map/pallas_call | solution.py:595
  44.0 0.7 %copy.13 = bf16[128,1024]{1,0:T(8,128)(2,1)} copy(bf16[128,1024]{1,0:T(8,128)(2,1)S(1)} %shard_map.109) | data formatting | bytes 524288

commit v8 on v6

--- a/solution.py
+++ b/solution.py
@@ -199,7 +199,7 @@
     edges = []
     for step, mate in enumerate(mates):
         copy = pltpu.make_async_remote_copy(
-            src_ref=edge_sum,
+            src_ref=edge_sum.at[pl.ds(0, 8)],
             dst_ref=edge_sums.at[step],
             send_sem=edge_send.at[step],
             recv_sem=edge_recv.at[step],
@@ -230,7 +230,7 @@
     first_row = edge_sum[0:8, :]
     for step, copy in enumerate(edges):
         copy.wait_recv()
-        first_row = first_row + edge_sums[step, 0:8, :]
+        first_row = first_row + edge_sums[step]
     first_row = cat([jnp.tanh(first_row[:1, :128]), first_row[:1, 128:]], 1)
     for copy in spread:
         copy.wait_recv()
@@ -330,16 +330,16 @@
         a_kk = [jnp.where(strict, scores[h][:, :T], 0.0) for h in H]
         low = [jnp.where(strict, scores[h][:, T:], 0.0) for h in H]
 
-        @pl.when(g == 1)
-        def _():
-            forward(0)
-
         inv = unit_inverse(low, row, col)
         kv = [dot(cat(split(a_kk[h]), 1), cat([valv[h // 2]] * 2, 0)) for h in H]
         right = [
             cat([dir_in[p] * e_mid[p], jnp.where(first, kv[2 * p], kv[2 * p + 1])], 1) for p in P
         ]
         sol = [mm3(inv[h], right[h // 2]) for h in H]
+        @pl.when(g == 1)
+        def _():
+            forward(0)
+
         low_lane = iota((64, 128), 1) < 64
         solved = [jnp.where(first2, sol[2 * p], sol[2 * p + 1]) for p in P]
         ends = [split(cat([-rem_out[p] * e_end[p], key_out[p] * e_end[p]], 0).T) for p in P]
@@ -591,7 +591,7 @@
             dma((2 * nhead,)),
             dma((2 * nhead,)),
             vm((16, 256), F32),
-            vm((nhead - 1, 16, 256), F32),
+            vm((nhead - 1, 8, 256), F32),
             vm((T, 256), BF16),
             dma((nhead - 1,)),
             dma((nhead - 1,)),

time: 44.8 us -> 44.8 us (level); the launches traced: 44.7 us -> 44.3 us
    pallas_call x1, Pallas kernels: 44 us -> 43.6 us  [mixed_of(): pl.pallas_call(functools.partial(mixed_kernel, nctx=nctx, nhead=nhead), i...]
where the time goes in v8:
time: 44.8 us; the launch traced here: 44.3 us
  Pallas kernels  43.6 us (97%)
  local copies, waits for them, and re-layouts  0.71 us (2%)
    pallas_call x1, Pallas kernels, mixed_of(): pl.pallas_call(functools.partial(mixed_kernel, nctx=nctx, nhead=nhead), i...  43.6 us

profile of v8, /device:TPU:25, one launch (start us, length us, event | category | flops | bytes accessed | tf_op | source)
XLA Modules:
  0.0 44.3 jit_solution(1623482412793160221)
XLA Ops:
  0.0 43.6 %shard_map.109 = bf16[128,1024]{1,0:T(8,128)(2,1)S(1)} custom-call(bf16[128,1024]{1,0:T(8,128)(2,1)} %x_h.1, f32[1,1024]{1,0:T(1,128)} %bitcast.3, bf16[1024,256]{1,0:T(8,128)(2,1)} %down_h.1, bf16[128,1024]{1,0:T(8,128)(2,1)} %du_h.1, bf16[128,1024]{1,0:T(8,128)(2,1)} %ru_h.1, f32[1,1024]{1,0:T(1,128)} %bitcast.4, f32[1,1024]{1,0:T(1,128)} %bitcast.5, ...), custom_call_target="tpu_custom_call" | custom-call | tf_op jit(solution)/shard_map/pallas_call | solution.py:579
  43.6 0.7 %copy.13 = bf16[128,1024]{1,0:T(8,128)(2,1)} copy(bf16[128,1024]{1,0:T(8,128)(2,1)S(1)} %shard_map.109) | data formatting | bytes 524288
